TPU v7x, 1024 devices: a whole 4x4x32 slice. The times are simulated.
1024 devices in a mesh: sub: 64 (over z, core), dom: 16 (over y, x).
Axes of the slice: x: 4, y: 4, z: 32, core: 2. Of those that a mesh axis runs over, the one named last changes fastest.
Arguments:
- loads: float32 [64, 16, 1024, 128], P('sub', 'dom'), may hold values from -6 to 6
- coefficient: float32 [64, 16], P('sub', 'dom'), may hold values from 0.5 to 4
- schur_ref: bfloat16 [1024, 1024], replicated, as said below
- schur_inverse: bfloat16 [64, 16, 1024, 1024], P('sub', 'dom'), as said below
- coarse_basis: bfloat16 [64, 16, 1024, 96], P('sub', 'dom'), may hold values from -0.1875 to 0.1875
- partners: int32 [64, 16, 2, 8], P('sub', 'dom'), may hold values from 0 to 15
- routes: int32 [64, 16, 96, 1], P('sub', 'dom'), may hold values from 0 to 63; in each aligned block of 96 rows (0 to 95, 96 to 191, ..., all dimensions but the last counted through in order) at most 2 rows name the same one
- coarse_rows: int32 [64, 16, 96], P('sub', 'dom'), may hold values from 0 to 63
- primal_count: int32 [64, 16], P('sub', 'dom'), may hold values from 48 to 96
- coarse_inverse: float32 [64, 16, 64, 64], P('sub', 'dom'), as said below
Outputs:
- solution: float32 [64, 16, 1024, 128], P('sub', 'dom')
Inputs may be any that keep to these rules, and one draw needn't show every extreme that they name: `routes`: among the 96 listed primal rows of one subdomain at most 2 name one coarse group, and some subdomain has exactly 2 for some group. `schur_ref`: symmetric and positive definite. `schur_inverse`: each block symmetric and positive definite. `coarse_inverse`: each block symmetric and positive definite.
All inputs are finite; a program needn't handle non-finite values.
Results may differ from a plain program's by a relative error of at most 0.0012.
Values sent between devices are 32-bit elements; how exact they have to be, the bound alone decides.
No kernel may reach another device: no remote copies, remote signals or barrier semaphores. Data moves between devices by JAX's collectives and lax.ppermute only.
A program may use at most 32 MiB of HBM per device.

v0:
```python
import jax
import jax.numpy as jnp
from jax import lax
from jax.sharding import PartitionSpec as P

TILE = 128
ITERS = 2


exact_mode = lax.Precision.HIGHEST


def body(
    loads,
    coefficient,
    schur_ref,
    schur_inverse,
    coarse_basis,
    partners,
    routes,
    coarse_rows,
    primal_count,
    coarse_inverse,
):
    rows_total = loads.shape[2]
    columns = loads.shape[3]
    tile_count = rows_total // TILE
    members = lax.axis_size("dom")
    groups = lax.axis_size("sub")
    tile_cap = (tile_count + members - 2) // (members - 1)
    primal_max = coarse_basis.shape[3]
    primal_cap = max(2, (primal_max + groups - 1) // groups)
    coarse_size = coarse_inverse.shape[3]
    peer_dev = partners[0, 0, 0]
    pair_id = partners[0, 0, 1]
    earlier = (peer_dev[None, :] == peer_dev[:, None]) & (pair_id[None, :] < pair_id[:, None])
    slot_idx = peer_dev * tile_cap + jnp.sum(earlier.astype(jnp.int32), axis=1)
    slot_match = jnp.arange(members * tile_cap, dtype=jnp.int32)[:, None] == slot_idx[None, :]
    tile_ids = jnp.arange(tile_count, dtype=jnp.int32)
    slot_source = jnp.sum(jnp.where(slot_match, tile_ids[None, :], 0), axis=1)
    slot_used = jnp.any(slot_match, axis=1).astype(jnp.float32)

    def assemble(vector):
        tile_rows = vector.reshape(tile_count, TILE, columns)
        outgoing = tile_rows[slot_source] * slot_used[:, None, None]
        incoming = lax.all_to_all(outgoing, "dom", split_axis=0, concat_axis=0, tiled=True)
        mirrored = incoming[slot_idx]
        return vector + mirrored.reshape(rows_total, columns)

    primal_pos = jnp.arange(primal_max, dtype=jnp.int32)
    live_flag = primal_pos < primal_count[0, 0]
    live_rows = live_flag.astype(jnp.float32)
    target = routes[0, 0, :, 0]
    ahead = (target[None, :] == target[:, None]) & (primal_pos[None, :] < primal_pos[:, None])
    primal_slot = target * primal_cap + jnp.sum(ahead.astype(jnp.int32), axis=1)
    send_mask = jnp.arange(groups * primal_cap, dtype=jnp.int32)[:, None] == primal_slot[None, :]
    send_table = send_mask.astype(jnp.float32)
    row_labels = jnp.where(live_flag, coarse_rows[0, 0] + 1, 0)
    labels = jnp.sum(jnp.where(send_mask, row_labels[None, :], 0), axis=1)
    basis_wide = coarse_basis[0, 0].astype(jnp.float32)
    inverse_local = schur_inverse[0, 0]
    coarse_block = coarse_inverse[0, 0]
    stiffness = coefficient[0, 0]
    coarse_ids = jnp.arange(coarse_size, dtype=jnp.int32)

    def precondition(residual):
        primal = (
            jnp.einsum("ip,ik->pk", basis_wide, 0.5 * residual, precision=exact_mode)
            * live_rows[:, None]
        )
        outgoing = jnp.dot(send_table, primal, precision=exact_mode)
        values_in, labels_in = (
            lax.all_to_all(outgoing, "sub", split_axis=0, concat_axis=0, tiled=True),
            lax.all_to_all(labels, "sub", split_axis=0, concat_axis=0, tiled=True),
        )
        owner_table = (labels_in[:, None] - 1 == coarse_ids[None, :]).astype(jnp.float32)
        coarse = jnp.einsum("sc,sk->ck", owner_table, values_in, precision=exact_mode)
        solved = jnp.dot(coarse_block, coarse, precision=exact_mode)
        answer = jnp.dot(owner_table, solved, precision=exact_mode)
        returned = lax.all_to_all(answer, "sub", split_axis=0, concat_axis=0, tiled=True)
        picked = (
            jnp.einsum("sp,sk->pk", send_table, returned, precision=exact_mode) * live_rows[:, None]
        )
        local_part = 0.25 * jnp.dot(
            inverse_local, residual.astype(jnp.bfloat16), preferred_element_type=jnp.float32
        )
        return assemble(local_part + jnp.dot(basis_wide, picked, precision=exact_mode))

    residual = assemble(loads[0, 0])
    solution = jnp.zeros_like(residual)

    def column_dot(left, right, weight):
        return lax.psum(weight * jnp.sum(left * right, axis=0), ("sub", "dom"))

    precond = precondition(residual)
    direction = precond
    energy = column_dot(residual, precond, 0.5)
    for iteration in range(ITERS):
        product = stiffness * jnp.dot(
            schur_ref, direction.astype(jnp.bfloat16), preferred_element_type=jnp.float32
        )
        applied = assemble(product)
        step_size = energy / column_dot(direction, applied, 0.5)
        solution = solution + step_size * direction
        if iteration + 1 < ITERS:
            residual = residual - step_size * applied
            precond = precondition(residual)
            renewed = column_dot(residual, precond, 0.5)
            direction = precond + renewed / energy * direction
            energy = renewed
    return solution.reshape(1, 1, rows_total, columns)


def solution(mesh):
    return jax.shard_map(
        body,
        mesh=mesh,
        in_specs=(
            P("sub", "dom", None, None),
            P("sub", "dom"),
            P(),
            P("sub", "dom", None, None),
            P("sub", "dom", None, None),
            P("sub", "dom", None, None),
            P("sub", "dom", None, None),
            P("sub", "dom", None),
            P("sub", "dom"),
            P("sub", "dom", None, None),
        ),
        out_specs=P("sub", "dom", None, None),
        check_vma=False,
    )
```

profile of v0, /device:TPU:1, one launch (start us, length us, event | category | flops | bytes accessed | tf_op | source)
XLA Modules:
  0.0 810.4 jit_solution(6050009583139121427)
XLA Ops:
  4.8 7.8 all-to-all-start
  14.3 10.5 %all-to-all-done = f32[16,128,128]{2,1,0:T(8,128)} async-done(((f32[16,128,128]{2,1,0:T(8,128)}), f32[16,128,128]{2,1,0:T(8,128)}, u32[]{:S(2)}, u32[]{:S(2)}) %all-to-all-start) | async-done | bytes 1048608 | tf_op jit(solution)/shard_map/all_to_all | solution.py:46
  24.8 35.3 %all-to-all-start.1 = ((s32[64,2,1]{1,2,0:T(1,128)}), s32[64,2,1]{1,2,0:T(1,128)S(1)}, u32[]{:S(2)}, u32[]{:S(2)}) async-start(s32[64,2,1]{1,2,0:T(1,128)} %bitcast.16), calls=%async_computation.1 | async-start | bytes 65536 | tf_op jit(solution)/shard_map/all_to_all | solution.py:74
  63.3 19.1 %all-to-all-done.1 = s32[64,2,1]{1,2,0:T(1,128)S(1)} async-done(((s32[64,2,1]{1,2,0:T(1,128)}), s32[64,2,1]{1,2,0:T(1,128)S(1)}, u32[]{:S(2)}, u32[]{:S(2)}) %all-to-all-start.1) | async-done | bytes 544 | tf_op jit(solution)/shard_map/all_to_all | solution.py:74
  82.4 5.8 all-to-all-start.2
  88.4 24.9 %all-to-all-done.2 = f32[64,2,128]{2,1,0:T(2,128)S(1)} async-done(((f32[64,2,128]{2,1,0:T(2,128)}), f32[64,2,128]{2,1,0:T(2,128)S(1)}, u32[]{:S(2)}, u32[]{:S(2)}) %all-to-all-start.2) | async-done | bytes 65568 | tf_op jit(solution)/shard_map/all_to_all | solution.py:73
  114.7 5.8 all-to-all-start.3
  122.1 23.5 %all-to-all-done.3 = f32[64,2,128]{2,1,0:T(2,128)S(1)} async-done(((f32[64,2,128]{2,1,0:T(2,128)}), f32[64,2,128]{2,1,0:T(2,128)S(1)}, u32[]{:S(2)}, u32[]{:S(2)}) %all-to-all-start.3) | async-done | bytes 65568 | tf_op jit(solution)/shard_map/all_to_all | solution.py:80
  148.4 2.7 gather_fusion.2
  151.1 2.4 broadcast_multiply_fusion.3
  153.4 4.3 all-to-all-start.4
  158.4 14.6 %all-to-all-done.4 = f32[16,128,128]{2,1,0:T(8,128)} async-done(((f32[16,128,128]{2,1,0:T(8,128)}), f32[16,128,128]{2,1,0:T(8,128)}, u32[]{:S(2)}, u32[]{:S(2)}) %all-to-all-start.4) | async-done | bytes 1048608 | tf_op jit(solution)/shard_map/all_to_all | solution.py:46
  177.1 3.2 fusion.13
  182.4 2.7 gather_fusion.4
  185.1 2.4 broadcast_multiply_fusion.2
  187.5 5.0 all-to-all-start.5
  195.6 11.9 %all-to-all-done.5 = f32[16,128,128]{2,1,0:T(8,128)} async-done(((f32[16,128,128]{2,1,0:T(8,128)}), f32[16,128,128]{2,1,0:T(8,128)}, u32[]{:S(2)}, u32[]{:S(2)}) %all-to-all-start.5) | async-done | bytes 1048608 | tf_op jit(solution)/shard_map/all_to_all | solution.py:46
  207.5 2.6 gather_fusion.5
  212.2 2.3 multiply_reduce_fusion.2
  214.5 153.1 %all-reduce = (f32[128]{0:T(128)S(1)}, f32[128]{0:T(128)S(1)}) all-reduce(f32[128]{0:T(128)S(1)} %broadcast_multiply_fusion.8, f32[128]{0:T(128)S(1)} %broadcast_multiply_fusion.7), channel_id=1, replica_groups=mesh['sub'=64,'dom'=16] {'sub','dom'}, use_global_device_ids=true, to_apply=%region_6.7 | all-reduce | flops 256 | bytes 2048 | tf_op jit(solution)/shard_map/psum | solution.py:93
  369.8 33.1 %all_to_all.83 = f32[64,2,128]{2,1,0:T(2,128)S(1)} all-to-all(f32[64,2,128]{2,1,0:T(2,128)S(1)} %bitcast.119), channel_id=1, replica_groups=mesh['sub'=64,'dom'=16] {'sub'}, dimensions={0} | all-to-all | bytes 131072 | tf_op jit(solution)/shard_map/all_to_all | solution.py:73
  404.2 5.9 all-to-all-start.7
  411.7 23.5 %all-to-all-done.7 = f32[64,2,128]{2,1,0:T(2,128)S(1)} async-done(((f32[64,2,128]{2,1,0:T(2,128)}), f32[64,2,128]{2,1,0:T(2,128)S(1)}, u32[]{:S(2)}, u32[]{:S(2)}) %all-to-all-start.7) | async-done | bytes 65568 | tf_op jit(solution)/shard_map/all_to_all | solution.py:80
  435.5 2.3 fusion.4
  439.8 2.6 gather_fusion.6
  443.8 19.5 %all_to_all.84 = f32[16,128,128]{2,1,0:T(8,128)} all-to-all(f32[16,128,128]{2,1,0:T(8,128)S(1)} %broadcast_multiply_fusion.1), channel_id=1, replica_groups=mesh['sub'=64,'dom'=16] {'dom'}, dimensions={0} | all-to-all | bytes 2097152 | tf_op jit(solution)/shard_map/all_to_all | solution.py:46
  463.3 2.6 gather_fusion.7
  470.0 151.7 %psum.30 = f32[128]{0:T(128)S(1)} all-reduce(f32[128]{0:T(128)S(1)} %broadcast_multiply_fusion.6), channel_id=1, replica_groups=mesh['sub'=64,'dom'=16] {'sub','dom'}, use_global_device_ids=true, to_apply=%region_10.11 | all-reduce | flops 128 | bytes 1024 | tf_op jit(solution)/shard_map/psum | solution.py:93
  621.7 3.4 fusion.12
  629.4 20.2 %all_to_all.85 = f32[16,128,128]{2,1,0:T(8,128)} all-to-all(f32[16,128,128]{2,1,0:T(8,128)S(1)} %broadcast_multiply_fusion), channel_id=1, replica_groups=mesh['sub'=64,'dom'=16] {'dom'}, dimensions={0} | all-to-all | bytes 2097152 | tf_op jit(solution)/shard_map/all_to_all | solution.py:46
  649.5 2.6 gather_fusion.9
  655.6 151.8 %psum.31 = f32[128]{0:T(128)S(1)} all-reduce(f32[128]{0:T(128)S(1)} %broadcast_multiply_fusion.5), channel_id=1, replica_groups=mesh['sub'=64,'dom'=16] {'sub','dom'}, use_global_device_ids=true, to_apply=%region_12.13 | all-reduce | flops 128 | bytes 1024 | tf_op jit(solution)/shard_map/psum | solution.py:93
  (84 shorter events, 49.6 us)
Async XLA Ops:
  0.0 120.5 %copy-start = (bf16[1,1,1024,1024]{3,2,1,0:T(8,128)(2,1)S(1)}, bf16[1,1,1024,1024]{3,2,1,0:T(8,128)(2,1)}, u32[]{:S(2)}) copy-start(bf16[1,1,1024,1024]{3,2,1,0:T(8,128)(2,1)} %param.13) | copy-start | bytes 6291460
  3.6 9.6 %copy-start.10 = (s32[1,1,96,1]{2,3,1,0:T(1,128)S(1)}, s32[1,1,96,1]{2,3,1,0:T(1,128)}, u32[]{:S(2)}) copy-start(s32[1,1,96,1]{2,3,1,0:T(1,128)} %param.16) | copy-start | bytes 1156
  3.6 9.8 %copy-start.9 = (s32[1,1,96]{2,1,0:T(1,128)S(1)}, s32[1,1,96]{2,1,0:T(1,128)}, u32[]{:S(2)}) copy-start(s32[1,1,96]{2,1,0:T(1,128)} %param.17) | copy-start | bytes 1156
  3.6 10.7 %copy-start.8 = (s32[1,1,2,8]{3,2,1,0:T(2,128)S(1)}, s32[1,1,2,8]{3,2,1,0:T(2,128)}, u32[]{:S(2)}) copy-start(s32[1,1,2,8]{3,2,1,0:T(2,128)} %param.15) | copy-start | bytes 196
  4.8 57.2 %copy-start.1 = (f32[1,1,1024,128]{3,2,1,0:T(8,128)S(1)}, f32[1,1,1024,128]{3,2,1,0:T(8,128)}, u32[]{:S(2)}) copy-start(f32[1,1,1024,128]{3,2,1,0:T(8,128)} %param.10) | copy-start | bytes 1572868
  4.8 57.2 %copy-start.6 = (bf16[1,1,1024,96]{2,3,1,0:T(8,128)(2,1)S(1)}, bf16[1,1,1024,96]{2,3,1,0:T(8,128)(2,1)}, u32[]{:S(2)}) copy-start(bf16[1,1,1024,96]{2,3,1,0:T(8,128)(2,1)} %param.14) | copy-start | bytes 589828
  4.8 108.9 %copy-start.7 = (f32[1,1,64,64]{3,2,1,0:T(8,128)S(1)}, f32[1,1,64,64]{3,2,1,0:T(8,128)}, u32[]{:S(2)}) copy-start(f32[1,1,64,64]{3,2,1,0:T(8,128)} %param.19) | copy-start | bytes 49156
  4.8 20.0 %all-to-all-start = ((f32[16,128,128]{2,1,0:T(8,128)}), f32[16,128,128]{2,1,0:T(8,128)}, u32[]{:S(2)}, u32[]{:S(2)}) async-start(f32[16,128,128]{2,1,0:T(8,128)} %broadcast_multiply_fusion.4), calls=%async_computation | async-start | bytes 2097152 | tf_op jit(solution)/shard_map/all_to_all | solution.py:46
  24.8 57.6 %all-to-all-start.1 = ((s32[64,2,1]{1,2,0:T(1,128)}), s32[64,2,1]{1,2,0:T(1,128)S(1)}, u32[]{:S(2)}, u32[]{:S(2)}) async-start(s32[64,2,1]{1,2,0:T(1,128)} %bitcast.16), calls=%async_computation.1 | async-start | bytes 65536 | tf_op jit(solution)/shard_map/all_to_all | solution.py:74
  61.9 60.2 %copy-start.2 = (f32[8,128,128]{2,1,0:T(8,128)}, f32[8,128,128]{2,1,0:T(8,128)S(1)}, u32[]{:S(2)}) copy-start(f32[8,128,128]{2,1,0:T(8,128)S(1)} %gather_fusion.1) | copy-start | bytes 1572868
  82.4 31.0 %all-to-all-start.2 = ((f32[64,2,128]{2,1,0:T(2,128)}), f32[64,2,128]{2,1,0:T(2,128)S(1)}, u32[]{:S(2)}, u32[]{:S(2)}) async-start(f32[64,2,128]{2,1,0:T(2,128)} %bitcast.19), calls=%async_computation.2 | async-start | bytes 131072 | tf_op jit(solution)/shard_map/all_to_all | solution.py:73
  114.7 31.0 %all-to-all-start.3 = ((f32[64,2,128]{2,1,0:T(2,128)}), f32[64,2,128]{2,1,0:T(2,128)S(1)}, u32[]{:S(2)}, u32[]{:S(2)}) async-start(f32[64,2,128]{2,1,0:T(2,128)} %bitcast.22), calls=%async_computation.3 | async-start | bytes 131072 | tf_op jit(solution)/shard_map/all_to_all | solution.py:80
  147.4 6.1 copy-start.4
  153.4 19.6 %all-to-all-start.4 = ((f32[16,128,128]{2,1,0:T(8,128)}), f32[16,128,128]{2,1,0:T(8,128)}, u32[]{:S(2)}, u32[]{:S(2)}) async-start(f32[16,128,128]{2,1,0:T(8,128)} %broadcast_multiply_fusion.3), calls=%async_computation.4 | async-start | bytes 2097152 | tf_op jit(solution)/shard_map/all_to_all | solution.py:46
  187.5 20.1 %all-to-all-start.5 = ((f32[16,128,128]{2,1,0:T(8,128)}), f32[16,128,128]{2,1,0:T(8,128)}, u32[]{:S(2)}, u32[]{:S(2)}) async-start(f32[16,128,128]{2,1,0:T(8,128)} %broadcast_multiply_fusion.2), calls=%async_computation.5 | async-start | bytes 2097152 | tf_op jit(solution)/shard_map/all_to_all | solution.py:46
  193.5 18.7 %copy-start.5 = (f32[1,1,1024,128]{2,3,1,0:T(8,128)S(1)}, f32[1,1,1024,128]{2,3,1,0:T(8,128)}, u32[]{:S(2)}) copy-start(f32[1,1,1024,128]{2,3,1,0:T(8,128)} %copy.37) | copy-start | bytes 1572868
  404.2 31.0 %all-to-all-start.7 = ((f32[64,2,128]{2,1,0:T(2,128)}), f32[64,2,128]{2,1,0:T(2,128)S(1)}, u32[]{:S(2)}, u32[]{:S(2)}) async-start(f32[64,2,128]{2,1,0:T(2,128)} %bitcast.33), calls=%async_computation.7 | async-start | bytes 131072 | tf_op jit(solution)/shard_map/all_to_all | solution.py:80
  629.4 24.8 %copy-start.3 = (f32[1024,128]{0,1:T(8,128)S(1)}, f32[1024,128]{0,1:T(8,128)}, u32[]{:S(2)}) copy-start(f32[1024,128]{0,1:T(8,128)} %get-tuple-element.10) | copy-start | bytes 1572868
where the time goes:
time: 813 us; the launch traced here: 810 us
  blocking collectives  529 us (65%)
  waiting for transfers between devices  128 us (16%)
  starting transfers between devices  69.9 us (9%)
  local copies, waits for them, and re-layouts  43 us (5%)
  other arithmetic  19.6 us (2%)
  matrix products  18.8 us (2%)
    psum x3, blocking collectives, column_dot(): return lax.psum(weight * jnp.sum(left * right, axis=0), ('sub', 'dom'))  457 us
    all_to_all x2, waiting for transfers between devices, precondition(): lax.all_to_all(answer, 'sub', split_axis=0, concat_axis=0, tiled=True)  47.1 us
    all_to_all x2, blocking collectives, assemble(): lax.all_to_all(outgoing, 'dom', split_axis=0, concat_axis=0, tiled=True)  39.7 us
    all_to_all x3, waiting for transfers between devices, assemble(): lax.all_to_all(outgoing, 'dom', split_axis=0, concat_axis=0, tiled=True)  37 us
    all_to_all x1, starting transfers between devices, precondition(): lax.all_to_all(labels, 'sub', split_axis=0, concat_axis=0, tiled=True)  35.3 us
    all_to_all x1, blocking collectives, precondition(): lax.all_to_all(outgoing, 'sub', split_axis=0, concat_axis=0, tiled=True)  33.1 us
    all_to_all x1, waiting for transfers between devices, precondition(): lax.all_to_all(outgoing, 'sub', split_axis=0, concat_axis=0, tiled=True)  24.9 us
    all_to_all x1, waiting for transfers between devices, precondition(): lax.all_to_all(labels, 'sub', split_axis=0, concat_axis=0, tiled=True)  19.1 us
  transfers between devices with their start and end apart: 7, of which 7 were waited for; matrix products, arithmetic and copies ran while one was open for 1% of the time, Pallas kernels for 0%

commit v1 on v0

v1 whole, which is shorter than its diff:
```python
import jax
import jax.numpy as jnp
from jax import lax
from jax.sharding import PartitionSpec as P

TILE = 128


def two_parts(value):
    high = lax.reduce_precision(value, 8, 7)
    low = value - high
    return jnp.concatenate([high, low], axis=1).astype(jnp.bfloat16)


def product(matrix, value, transposed=False):
    columns = value.shape[1]
    contract = ((0,), (0,)) if transposed else ((1,), (0,))
    both = lax.dot_general(
        matrix, two_parts(value), (contract, ((), ())), preferred_element_type=jnp.float32
    )
    return both[:, :columns] + both[:, columns:]


def body(
    loads,
    coefficient,
    schur_ref,
    schur_inverse,
    coarse_basis,
    partners,
    routes,
    coarse_rows,
    primal_count,
    coarse_inverse,
):
    rows_total = loads.shape[2]
    columns = loads.shape[3]
    peer_dev = partners[0, 0, 0]
    tile_count = peer_dev.shape[0]
    tile = rows_total // tile_count
    members = lax.axis_size("dom")
    groups = lax.axis_size("sub")
    primal_max = coarse_basis.shape[3]
    primal_cap = max(2, (primal_max + groups - 1) // groups)
    slots = groups * primal_cap
    coarse_size = coarse_inverse.shape[3]

    slot_match = jnp.arange(members, dtype=jnp.int32)[:, None] == peer_dev[None, :]
    tile_ids = jnp.arange(tile_count, dtype=jnp.int32)
    slot_source = jnp.sum(jnp.where(slot_match, tile_ids[None, :], 0), axis=1)

    def assemble(vector):
        tiles = vector.reshape(tile_count, tile, columns)
        incoming = lax.all_to_all(tiles[slot_source], "dom", 0, 0, tiled=True)
        return vector + incoming[peer_dev].reshape(rows_total, columns)

    primal_pos = jnp.arange(primal_max, dtype=jnp.int32)
    live = primal_pos < primal_count[0, 0]
    target = routes[0, 0, :, 0]
    ahead = (target[None, :] == target[:, None]) & (primal_pos[None, :] < primal_pos[:, None])
    primal_slot = target * primal_cap + jnp.sum(ahead.astype(jnp.int32), axis=1)
    send_mask = jnp.arange(slots, dtype=jnp.int32)[:, None] == primal_slot[None, :]
    send_mask = send_mask & live[None, :]
    labels = jnp.sum(jnp.where(send_mask, coarse_rows[0, 0][None, :] + 1, 0), axis=1)
    slot_basis = lax.dot_general(
        coarse_basis[0, 0],
        send_mask.astype(jnp.bfloat16),
        (((1,), (1,)), ((), ())),
        preferred_element_type=jnp.float32,
    ).astype(jnp.bfloat16)
    label_rows = jnp.pad(
        labels.reshape(groups, 1, primal_cap).astype(jnp.float32),
        ((0, 0), (0, 0), (0, columns - primal_cap)),
    )
    inverse_local = schur_inverse[0, 0]
    stiffness = coefficient[0, 0]
    coarse_ids = jnp.arange(coarse_size, dtype=jnp.int32).astype(jnp.float32)
    exact = lax.Precision.HIGHEST

    def shift(values):
        return lax.all_to_all(values, "sub", 0, 0, tiled=True)

    def primal_of(residual):
        return product(slot_basis, 0.5 * residual, True).reshape(groups, primal_cap, columns)

    def lifted(answer, residual):
        returned = shift(answer.reshape(groups, primal_cap, columns)).reshape(slots, columns)
        return 0.25 * product(inverse_local, residual) + product(slot_basis, returned)

    residual = assemble(loads[0, 0])
    arrived = shift(jnp.concatenate([primal_of(residual), label_rows], axis=1))
    labels_in = arrived[:, primal_cap, :primal_cap].reshape(slots)
    owner = (labels_in[:, None] - 1.0 == coarse_ids[None, :]).astype(jnp.float32)
    coupling = jnp.dot(
        jnp.dot(owner, coarse_inverse[0, 0], precision=exact), owner.T, precision=exact
    )
    values = arrived[:, :primal_cap].reshape(slots, columns)
    half_first = lifted(jnp.dot(coupling, values, precision=exact), residual)
    first = assemble(half_first)
    energy = jnp.sum(residual * half_first, axis=0)

    half_image = stiffness * product(schur_ref, first)
    image = assemble(half_image)
    gram_first = jnp.sum(first * half_image, axis=0)
    values = shift(primal_of(image)).reshape(slots, columns)
    half_second = lifted(jnp.dot(coupling, values, precision=exact), image)
    second = assemble(half_second)
    gram_mixed = jnp.sum(image * half_second, axis=0)
    gram_second = stiffness * jnp.sum(second * product(schur_ref, second), axis=0)

    sums = jnp.stack([energy, gram_first, gram_mixed, gram_second])
    sums = jnp.sum(shift(jnp.broadcast_to(sums[None], (groups, 4, columns))), axis=0)
    spread = jnp.broadcast_to(sums[None], (members, 4, columns))
    sums = jnp.sum(lax.all_to_all(spread, "dom", 0, 0, tiled=True), axis=0)
    energy, gram_first, gram_mixed, gram_second = sums[0], sums[1], sums[2], sums[3]

    step_first = energy / gram_first
    mixed_share = gram_mixed / gram_first
    step_second = (gram_mixed - gram_first / energy * gram_first) / (
        gram_second - mixed_share * gram_mixed
    )
    along_first = step_first + step_second * (step_first * mixed_share)
    along_second = step_second * step_first
    solution = along_first * first - along_second * second
    return solution.reshape(1, 1, rows_total, columns)


def solution(mesh):
    return jax.shard_map(
        body,
        mesh=mesh,
        in_specs=(
            P("sub", "dom", None, None),
            P("sub", "dom"),
            P(),
            P("sub", "dom", None, None),
            P("sub", "dom", None, None),
            P("sub", "dom", None, None),
            P("sub", "dom", None, None),
            P("sub", "dom", None),
            P("sub", "dom"),
            P("sub", "dom", None, None),
        ),
        out_specs=P("sub", "dom", None, None),
        check_vma=False,
    )
```

time: 813 us -> 336 us (0.41)
  blocking collectives: 529 us -> 120 us
  waiting for transfers between devices: 128 us -> 101 us
  local copies, waits for them, and re-layouts: 43 us -> 30.4 us
  starting transfers between devices: 69.9 us -> 58.7 us
  matrix products: 18.8 us -> 10.2 us
    psum x3 -> x0, blocking collectives: 457 us -> none  [column_dot(): return lax.psum(weight * jnp.sum(left * right, axis=0), ('sub', 'dom'))]
    all_to_all x3 -> x5, blocking collectives: 72.7 us -> 120 us  [the longest x2 69.9 us: shift(): return lax.all_to_all(values, 'sub', 0, 0, tiled=True)]
    all_to_all x7 -> x5, waiting for transfers between devices: 128 us -> 101 us  [the longest x3 76.5 us: shift(): return lax.all_to_all(values, 'sub', 0, 0, tiled=True)]
    all_to_all x7 -> x5, starting transfers between devices: 69.9 us -> 58.7 us  [the longest x3 46.6 us: shift(): return lax.all_to_all(values, 'sub', 0, 0, tiled=True)]
    reshape x9 -> x7, local copies, waits for them, and re-layouts: 15.5 us -> 6.62 us  [the longest x4 3.98 us: assemble(): return vector + incoming[peer_dev].reshape(rows_total, columns)]
    mul x9 -> x3, other arithmetic: 8.69 us -> 0.03 us  [the longest x2 0.02 us: body(): solution = along_first * first - along_second * second]
    dot_general x18 -> x13, matrix products: 18.8 us -> 10.2 us  [the longest x8 7.27 us: product(): lax.dot_general(matrix, two_parts(value), (contract, ((), ())), preferred...]
    gather x10 -> x8, local copies, waits for them, and re-layouts: 22.7 us -> 14.8 us  [the longest x4 7.54 us: assemble(): incoming = lax.all_to_all(tiles[slot_source], 'dom', 0, 0, tiled=True)]
  transfers between devices with their start and end apart: 7 -> 5, of which waited for: 7 -> 5; matrix products, arithmetic and copies ran while one was open for 1% -> 2% of each run, Pallas kernels for 0% -> 0%
where the time goes in v1:
time: 336 us; the launch traced here: 334 us
  blocking collectives  120 us (36%)
  waiting for transfers between devices  101 us (30%)
  starting transfers between devices  58.7 us (17%)
  local copies, waits for them, and re-layouts  30.4 us (9%)
  other arithmetic  12.7 us (4%)
  matrix products  10.2 us (3%)
    all_to_all x3, waiting for transfers between devices, shift(): return lax.all_to_all(values, 'sub', 0, 0, tiled=True)  76.5 us
    all_to_all x2, blocking collectives, shift(): return lax.all_to_all(values, 'sub', 0, 0, tiled=True)  69.9 us
    all_to_all x3, starting transfers between devices, shift(): return lax.all_to_all(values, 'sub', 0, 0, tiled=True)  46.6 us
    all_to_all x2, blocking collectives, assemble(): incoming = lax.all_to_all(tiles[slot_source], 'dom', 0, 0, tiled=True)  40.7 us
    all_to_all x2, waiting for transfers between devices, assemble(): incoming = lax.all_to_all(tiles[slot_source], 'dom', 0, 0, tiled=True)  24.2 us
    all_to_all x2, starting transfers between devices, assemble(): incoming = lax.all_to_all(tiles[slot_source], 'dom', 0, 0, tiled=True)  12.1 us
    all_to_all x1, blocking collectives, body(): sums = jnp.sum(lax.all_to_all(spread, 'dom', 0, 0, tiled=True), axis=0)  8.99 us
    gather x4, local copies, waits for them, and re-layouts, assemble(): incoming = lax.all_to_all(tiles[slot_source], 'dom', 0, 0, tiled=True)  7.54 us
  transfers between devices with their start and end apart: 5, of which 5 were waited for; matrix products, arithmetic and copies ran while one was open for 2% of the time, Pallas kernels for 0%

profile of v1, /device:TPU:1, one launch (start us, length us, event | category | flops | bytes accessed | tf_op | source)
XLA Modules:
  0.0 334.1 jit_solution(13305379198836730798)
XLA Ops:
  0.9 2.7 gather_fusion
  3.7 7.8 %all-to-all-start = ((f32[16,128,128]{2,1,0:T(8,128)}), f32[16,128,128]{2,1,0:T(8,128)}, u32[]{:S(2)}, u32[]{:S(2)}) async-start(f32[16,128,128]{2,1,0:T(8,128)} %gather_fusion), calls=%async_computation | async-start | bytes 2097152 | tf_op jit(solution)/shard_map/all_to_all | solution.py:54
  12.9 1.3 convolution_convert_fusion
  14.1 9.6 %all-to-all-done = f32[16,128,128]{2,1,0:T(8,128)} async-done(((f32[16,128,128]{2,1,0:T(8,128)}), f32[16,128,128]{2,1,0:T(8,128)}, u32[]{:S(2)}, u32[]{:S(2)}) %all-to-all-start) | async-done | bytes 1048608 | tf_op jit(solution)/shard_map/all_to_all | solution.py:54
  23.7 1.8 gather_fusion.1
  26.5 1.8 reduce-precision_convert_fusion.5
  29.5 35.3 %all-to-all-start.1 = ((f32[64,3,128]{2,1,0:T(4,128)}), f32[64,3,128]{2,1,0:T(4,128)S(1)}, u32[]{:S(2)}, u32[]{:S(2)}) async-start(f32[64,3,128]{2,1,0:T(4,128)} %pad_maximum_fusion), calls=%async_computation.1 | async-start | bytes 262144 | tf_op jit(solution)/shard_map/all_to_all | solution.py:81
  64.8 30.7 %all-to-all-done.1 = f32[64,3,128]{2,1,0:T(4,128)S(1)} async-done(((f32[64,3,128]{2,1,0:T(4,128)}), f32[64,3,128]{2,1,0:T(4,128)S(1)}, u32[]{:S(2)}, u32[]{:S(2)}) %all-to-all-start.1) | async-done | bytes 98336 | tf_op jit(solution)/shard_map/all_to_all | solution.py:81
  100.2 5.7 %all-to-all-start.2 = ((f32[64,2,128]{2,1,0:T(2,128)}), f32[64,2,128]{2,1,0:T(2,128)S(1)}, u32[]{:S(2)}, u32[]{:S(2)}) async-start(f32[64,2,128]{2,1,0:T(2,128)} %copy.80), calls=%async_computation.2 | async-start | bytes 131072 | tf_op jit(solution)/shard_map/all_to_all | solution.py:81
  105.9 1.7 fusion.4
  107.7 23.4 %all-to-all-done.2 = f32[64,2,128]{2,1,0:T(2,128)S(1)} async-done(((f32[64,2,128]{2,1,0:T(2,128)}), f32[64,2,128]{2,1,0:T(2,128)S(1)}, u32[]{:S(2)}, u32[]{:S(2)}) %all-to-all-start.2) | async-done | bytes 65568 | tf_op jit(solution)/shard_map/all_to_all | solution.py:81
  132.8 1.6 gather_fusion.2
  134.4 4.3 %all-to-all-start.3 = ((f32[16,128,128]{2,1,0:T(8,128)}), f32[16,128,128]{2,1,0:T(8,128)}, u32[]{:S(2)}, u32[]{:S(2)}) async-start(f32[16,128,128]{2,1,0:T(8,128)} %gather_fusion.2), calls=%async_computation.3 | async-start | bytes 2097152 | tf_op jit(solution)/shard_map/all_to_all | solution.py:54
  139.4 14.6 %all-to-all-done.3 = f32[16,128,128]{2,1,0:T(8,128)} async-done(((f32[16,128,128]{2,1,0:T(8,128)}), f32[16,128,128]{2,1,0:T(8,128)}, u32[]{:S(2)}, u32[]{:S(2)}) %all-to-all-start.3) | async-done | bytes 1048608 | tf_op jit(solution)/shard_map/all_to_all | solution.py:54
  154.0 1.8 gather_fusion.3
  156.8 1.3 reduce-precision_convert_fusion.3
  160.3 1.2 copy.101
  161.5 1.6 gather_fusion.4
  163.1 20.7 %all_to_all.50 = f32[16,128,128]{2,1,0:T(8,128)} all-to-all(f32[16,128,128]{2,1,0:T(8,128)} %gather_fusion.4), channel_id=1, replica_groups=mesh['sub'=64,'dom'=16] {'dom'}, dimensions={0} | all-to-all | bytes 2097152 | tf_op jit(solution)/shard_map/all_to_all | solution.py:54
  183.8 1.8 gather_fusion.5
  186.6 2.0 reduce-precision_convert_fusion.2
  189.7 33.1 %all_to_all.51 = f32[64,2,128]{2,1,0:T(2,128)S(1)} all-to-all(f32[64,2,128]{2,1,0:T(2,128)S(1)} %bitcast.98), channel_id=1, replica_groups=mesh['sub'=64,'dom'=16] {'sub'}, dimensions={0} | all-to-all | bytes 131072 | tf_op jit(solution)/shard_map/all_to_all | solution.py:81
  223.7 5.7 %all-to-all-start.6 = ((f32[64,2,128]{2,1,0:T(2,128)}), f32[64,2,128]{2,1,0:T(2,128)S(1)}, u32[]{:S(2)}, u32[]{:S(2)}) async-start(f32[64,2,128]{2,1,0:T(2,128)} %copy.88), calls=%async_computation.6 | async-start | bytes 131072 | tf_op jit(solution)/shard_map/all_to_all | solution.py:81
  229.4 2.7 fusion.7
  232.2 22.4 %all-to-all-done.6 = f32[64,2,128]{2,1,0:T(2,128)S(1)} async-done(((f32[64,2,128]{2,1,0:T(2,128)}), f32[64,2,128]{2,1,0:T(2,128)S(1)}, u32[]{:S(2)}, u32[]{:S(2)}) %all-to-all-start.6) | async-done | bytes 65568 | tf_op jit(solution)/shard_map/all_to_all | solution.py:81
  258.0 1.6 gather_fusion.6
  259.6 20.0 %all_to_all.52 = f32[16,128,128]{2,1,0:T(8,128)} all-to-all(f32[16,128,128]{2,1,0:T(8,128)} %gather_fusion.6), channel_id=1, replica_groups=mesh['sub'=64,'dom'=16] {'dom'}, dimensions={0} | all-to-all | bytes 2097152 | tf_op jit(solution)/shard_map/all_to_all | solution.py:54
  279.6 1.8 gather_fusion.7
  282.4 1.4 reduce-precision_convert_fusion
  285.2 36.8 %all_to_all.53 = f32[64,4,128]{2,1,0:T(4,128)S(1)} all-to-all(f32[64,4,128]{2,1,0:T(4,128)S(1)} %broadcast_in_dim.32), channel_id=1, replica_groups=mesh['sub'=64,'dom'=16] {'sub'}, dimensions={0} | all-to-all | bytes 262144 | tf_op jit(solution)/shard_map/all_to_all | solution.py:81
  322.1 9.0 %all_to_all.54 = f32[16,4,128]{2,1,0:T(4,128)S(1)} all-to-all(f32[16,4,128]{2,1,0:T(4,128)S(1)} %broadcast_in_dim.33), channel_id=1, replica_groups=mesh['sub'=64,'dom'=16] {'dom'}, dimensions={0} | all-to-all | bytes 65536 | tf_op jit(solution)/shard_map/all_to_all | solution.py:114
  332.0 2.0 copy.95
  (81 shorter events, 23.2 us)
Async XLA Ops:
  0.0 105.9 %copy-start = (bf16[1,1,1024,1024]{3,2,1,0:T(8,128)(2,1)S(1)}, bf16[1,1,1024,1024]{3,2,1,0:T(8,128)(2,1)}, u32[]{:S(2)}) copy-start(bf16[1,1,1024,1024]{3,2,1,0:T(8,128)(2,1)} %param.13) | copy-start | bytes 6291460
  0.9 10.5 %copy-start.3 = (f32[1,1,1024,128]{3,2,1,0:T(8,128)S(1)}, f32[1,1,1024,128]{3,2,1,0:T(8,128)}, u32[]{:S(2)}) copy-start(f32[1,1,1024,128]{3,2,1,0:T(8,128)} %param.10) | copy-start | bytes 1572868
  3.7 8.6 %copy-start.9 = (s32[1,1,96]{2,1,0:T(1,128)S(1)}, s32[1,1,96]{2,1,0:T(1,128)}, u32[]{:S(2)}) copy-start(s32[1,1,96]{2,1,0:T(1,128)} %param.17) | copy-start | bytes 1156
  3.7 8.7 %copy-start.10 = (s32[1,1,96,1]{2,3,1,0:T(1,128)S(1)}, s32[1,1,96,1]{2,3,1,0:T(1,128)}, u32[]{:S(2)}) copy-start(s32[1,1,96,1]{2,3,1,0:T(1,128)} %param.16) | copy-start | bytes 1156
  3.7 9.2 %copy-start.8 = (s32[1,1,2,8]{3,2,1,0:T(2,128)S(1)}, s32[1,1,2,8]{3,2,1,0:T(2,128)}, u32[]{:S(2)}) copy-start(s32[1,1,2,8]{3,2,1,0:T(2,128)} %param.15) | copy-start | bytes 196
  3.7 20.0 %all-to-all-start = ((f32[16,128,128]{2,1,0:T(8,128)}), f32[16,128,128]{2,1,0:T(8,128)}, u32[]{:S(2)}, u32[]{:S(2)}) async-start(f32[16,128,128]{2,1,0:T(8,128)} %gather_fusion), calls=%async_computation | async-start | bytes 2097152 | tf_op jit(solution)/shard_map/all_to_all | solution.py:54
  28.3 77.6 %copy-start.6 = (bf16[1024,128]{0,1:T(8,128)(2,1)S(1)}, bf16[1024,128]{0,1:T(8,128)(2,1)}, u32[]{:S(2)}) copy-start(bf16[1024,128]{0,1:T(8,128)(2,1)} %get-tuple-element.20) | copy-start | bytes 786436
  29.5 66.0 %all-to-all-start.1 = ((f32[64,3,128]{2,1,0:T(4,128)}), f32[64,3,128]{2,1,0:T(4,128)S(1)}, u32[]{:S(2)}, u32[]{:S(2)}) async-start(f32[64,3,128]{2,1,0:T(4,128)} %pad_maximum_fusion), calls=%async_computation.1 | async-start | bytes 262144 | tf_op jit(solution)/shard_map/all_to_all | solution.py:81
  95.5 1.6 copy-start.7
  100.2 30.8 %all-to-all-start.2 = ((f32[64,2,128]{2,1,0:T(2,128)}), f32[64,2,128]{2,1,0:T(2,128)S(1)}, u32[]{:S(2)}, u32[]{:S(2)}) async-start(f32[64,2,128]{2,1,0:T(2,128)} %copy.80), calls=%async_computation.2 | async-start | bytes 131072 | tf_op jit(solution)/shard_map/all_to_all | solution.py:81
  131.1 1.2 copy-start.5
  134.4 19.6 %all-to-all-start.3 = ((f32[16,128,128]{2,1,0:T(8,128)}), f32[16,128,128]{2,1,0:T(8,128)}, u32[]{:S(2)}, u32[]{:S(2)}) async-start(f32[16,128,128]{2,1,0:T(8,128)} %gather_fusion.2), calls=%async_computation.3 | async-start | bytes 2097152 | tf_op jit(solution)/shard_map/all_to_all | solution.py:54
  156.8 1.7 copy-start.1
  223.7 30.8 %all-to-all-start.6 = ((f32[64,2,128]{2,1,0:T(2,128)}), f32[64,2,128]{2,1,0:T(2,128)S(1)}, u32[]{:S(2)}, u32[]{:S(2)}) async-start(f32[64,2,128]{2,1,0:T(2,128)} %copy.88), calls=%async_computation.6 | async-start | bytes 131072 | tf_op jit(solution)/shard_map/all_to_all | solution.py:81
  254.6 1.2 copy-start.4
  282.4 1.9 copy-start.2

commit v2 on v1

v2 whole, which is shorter than its diff:
```python
import functools

import jax
import jax.numpy as jnp
from jax import lax
from jax.experimental import pallas as pl
from jax.experimental.pallas import tpu as pltpu
from jax.sharding import PartitionSpec as P

F32 = jnp.float32
BF16 = jnp.bfloat16
VMEM = pl.BlockSpec(memory_space=pltpu.VMEM)
SMEM = pl.BlockSpec(memory_space=pltpu.SMEM)


def parts_of(value):
    high = value.astype(BF16)
    low = (value - high.astype(F32)).astype(BF16)
    return high, low


def dot(left, right):
    return jnp.dot(left, right, preferred_element_type=F32)


def product(matrix, value):
    columns = value.shape[1]
    both = dot(matrix, jnp.concatenate(parts_of(value), axis=1))
    return both[:, :columns] + both[:, columns:]


def spread(peers_ref, value, out_ref):
    tile = out_ref.shape[1]
    out_ref[...] = jnp.zeros_like(out_ref)
    for t in range(value.shape[0] // tile):
        out_ref[peers_ref[0, t]] = value[t * tile : (t + 1) * tile]


def mirrored(peers_ref, half_ref, incoming_ref, out_ref):
    tile = incoming_ref.shape[1]
    for t in range(half_ref.shape[0] // tile):
        rows = slice(t * tile, (t + 1) * tile)
        out_ref[rows] = half_ref[rows] + incoming_ref[peers_ref[0, t]]


def column_sum(value):
    return jnp.sum(value, axis=0, keepdims=True)


def send_loads_kernel(peers_ref, loads_ref, out_ref):
    spread(peers_ref, loads_ref[...], out_ref)


def first_residual_kernel(peers_ref, loads_ref, incoming_ref, basis_ref, labels_ref, residual_ref, out_ref):
    mirrored(peers_ref, loads_ref, incoming_ref, residual_ref)
    out_ref[...] = product(basis_ref[...], 0.5 * residual_ref[...]) + labels_ref[...]


def residual_kernel(peers_ref, half_ref, incoming_ref, basis_ref, residual_ref, out_ref):
    mirrored(peers_ref, half_ref, incoming_ref, residual_ref)
    out_ref[...] = product(basis_ref[...], 0.5 * residual_ref[...])


def local_kernel(inverse_ref, residual_ref, out_ref):
    out_ref[...] = 0.25 * product(inverse_ref[...], residual_ref[...])


def split_product(high, low, value):
    value_high, value_low = parts_of(value)
    return dot(
        jnp.concatenate([high, high, low], axis=1),
        jnp.concatenate([value_high, value_low, value_high], axis=0),
    )


def first_coarse_kernel(cap, stride, arrived_ref, block_ref, high_ref, low_ref, out_ref):
    slots, columns = out_ref.shape
    coarse_size = block_ref.shape[0]
    received = arrived_ref.shape[0]
    arrived = jnp.concatenate(parts_of(arrived_ref[...]), axis=1)
    slot = lax.broadcasted_iota(jnp.int32, (slots, received), 0)
    row = lax.broadcasted_iota(jnp.int32, (slots, received), 1)
    base = (slot // cap) * stride
    pick_value = (row == base + slot % cap).astype(F32).astype(BF16)
    pick_label = (row == base + cap).astype(F32).astype(BF16)
    values = dot(pick_value, arrived)
    values = values[:, :columns] + values[:, columns:]
    label_rows = dot(pick_label, arrived[:, :columns])
    lane = lax.broadcasted_iota(jnp.int32, (slots, columns), 1)
    own = lax.broadcasted_iota(jnp.int32, (slots, columns), 0) % cap
    labels = jnp.sum(jnp.where(lane == own, label_rows, 0.0), axis=1, keepdims=True)
    ids = lax.broadcasted_iota(jnp.int32, (slots, coarse_size), 1).astype(F32)
    owner = (labels - 1.0 == ids).astype(F32).astype(BF16)
    block_high, block_low = parts_of(block_ref[...])
    across = (((1,), (1,)), ((), ()))

    def composed(part):
        rows = dot(owner, part).astype(BF16)
        return lax.dot_general(rows, owner, across, preferred_element_type=F32).astype(BF16)

    high, low = composed(block_high), composed(block_low)
    high_ref[...] = high
    low_ref[...] = low
    out_ref[...] = split_product(high, low, values)


def coarse_kernel(high_ref, low_ref, values_ref, out_ref):
    out_ref[...] = split_product(high_ref[...], low_ref[...], values_ref[...])


def lift_kernel(peers_ref, basis_ref, returned_ref, local_ref, residual_ref, half_ref, out_ref, sum_ref):
    half = local_ref[...] + product(basis_ref[...], returned_ref[...])
    half_ref[...] = half
    spread(peers_ref, half, out_ref)
    sum_ref[...] = column_sum(residual_ref[...] * half)


def operate_kernel(peers_ref, stiffness_ref, half_ref, incoming_ref, schur_ref, vector_ref, image_ref, out_ref, sum_ref):
    mirrored(peers_ref, half_ref, incoming_ref, vector_ref)
    vector = vector_ref[...]
    image = stiffness_ref[0, 0] * product(schur_ref[...], vector)
    image_ref[...] = image
    spread(peers_ref, image, out_ref)
    sum_ref[...] = column_sum(vector * image)


def last_kernel(
    peers_ref, stiffness_ref, half_ref, incoming_ref, schur_ref, energy_ref, first_ref, mixed_ref, vector_ref, out_ref
):
    mirrored(peers_ref, half_ref, incoming_ref, vector_ref)
    vector = vector_ref[...]
    second = stiffness_ref[0, 0] * column_sum(vector * product(schur_ref[...], vector))
    sums = jnp.concatenate([energy_ref[...], first_ref[...], mixed_ref[...], second], axis=0)
    out_ref[...] = jnp.broadcast_to(sums[None], out_ref.shape)


def regroup_kernel(sums_ref, out_ref):
    out_ref[...] = jnp.broadcast_to(jnp.sum(sums_ref[...], axis=0)[None], out_ref.shape)


def combine_kernel(sums_ref, first_ref, second_ref, out_ref):
    sums = jnp.sum(sums_ref[...], axis=0)
    energy, gram_first, gram_mixed, gram_second = (sums[i : i + 1] for i in range(4))
    step_first = energy / gram_first
    mixed_share = gram_mixed / gram_first
    step_second = (gram_mixed - gram_first / energy * gram_first) / (
        gram_second - mixed_share * gram_mixed
    )
    along_first = step_first + step_second * (step_first * mixed_share)
    along_second = step_second * step_first
    out_ref[...] = along_first * first_ref[...] - along_second * second_ref[...]


def call(kernel, scalars, inputs, outputs, flops=0):
    moved = sum(x.size * x.dtype.itemsize for x in inputs)
    moved += sum(x.size * x.dtype.itemsize for x in outputs)
    single = len(outputs) == 1
    return pl.pallas_call(
        kernel,
        out_shape=outputs[0] if single else tuple(outputs),
        in_specs=[SMEM] * len(scalars) + [VMEM] * len(inputs),
        out_specs=VMEM if single else tuple([VMEM] * len(outputs)),
        compiler_params=pltpu.CompilerParams(vmem_limit_bytes=20 << 20),
        cost_estimate=pl.CostEstimate(flops=flops, bytes_accessed=moved, transcendentals=0),
    )(*scalars, *inputs)


def body(
    loads,
    coefficient,
    schur_ref,
    schur_inverse,
    coarse_basis,
    partners,
    routes,
    coarse_rows,
    primal_count,
    coarse_inverse,
):
    rows_total, columns = loads.shape[2:]
    peers = partners[0, 0]
    tile_count = peers.shape[1]
    tile = rows_total // tile_count
    members = lax.axis_size("dom")
    groups = lax.axis_size("sub")
    primal_max = coarse_basis.shape[3]
    cap = max(2, (primal_max + groups - 1) // groups)
    stride = cap + 1
    slots = groups * cap
    stiffness = coefficient
    load_tiles = loads[0, 0]
    inverse_local = schur_inverse[0, 0]

    def shaped(*shape, dtype=F32):
        return jax.ShapeDtypeStruct(shape, dtype)

    vector_shape = shaped(rows_total, columns)
    slot_shape = shaped(slots, columns)
    tiles_shape = shaped(members, tile, columns)
    sum_shape = shaped(1, columns)
    big = 4 * rows_total * rows_total * columns
    thin = 4 * rows_total * slots * columns

    def exchange(tiles):
        return lax.all_to_all(tiles, "dom", 0, 0, tiled=True)

    def shift(values, per_group):
        grouped = values.reshape(groups, 1, per_group * columns)
        return lax.all_to_all(grouped, "sub", 0, 0, tiled=True).reshape(groups * per_group, columns)

    cores = 2
    chips = groups // cores
    layers = [
        [(z * cores + k) * members + d for k in range(cores) for d in range(members)]
        for z in range(chips)
    ]
    lines = [list(line) for line in zip(*layers)]

    def gather(values, sets):
        return lax.all_to_all(values, ("sub", "dom"), 0, 0, tiled=True, axis_index_groups=sets)

    incoming = exchange(call(send_loads_kernel, [peers], [load_tiles], [tiles_shape]))

    primal_pos = jnp.arange(primal_max, dtype=jnp.int32)
    live = primal_pos < primal_count[0, 0]
    target = routes[0, 0, :, 0]
    ahead = (target[None, :] == target[:, None]) & (primal_pos[None, :] < primal_pos[:, None])
    rank = jnp.sum(ahead.astype(jnp.int32), axis=1)
    basis = coarse_basis[0, 0]

    def placed(per_group):
        wanted = jnp.where(live, target * per_group + rank, -1)
        return jnp.arange(groups * per_group, dtype=jnp.int32)[:, None] == wanted[None, :]

    def chosen(per_group, basis_first):
        table = placed(per_group).astype(BF16)
        pair = (basis, table) if basis_first else (table, basis)
        across = (((1,), (1,)), ((), ()))
        return lax.dot_general(*pair, across, preferred_element_type=F32).astype(BF16)

    row_labels = jnp.where(live, coarse_rows[0, 0] + 1, 0)
    labels = jnp.sum(jnp.where(placed(cap), row_labels[None, :], 0), axis=1)
    labels = jnp.pad(labels.reshape(groups, 1, cap), ((0, 0), (cap, stride - cap - 1), (0, columns - cap)))
    labels = labels.reshape(groups * stride, columns).astype(F32)
    lift_basis = chosen(cap, True)
    slot_basis = chosen(cap, False)
    wide_basis = chosen(stride, False)

    residual, outgoing = call(
        first_residual_kernel,
        [peers],
        [load_tiles, incoming, wide_basis, labels],
        [vector_shape, shaped(groups * stride, columns)],
        2 * thin,
    )
    arrived = shift(outgoing, stride)
    local = call(local_kernel, [], [inverse_local, residual], [vector_shape], big)
    high, low, answer = call(
        functools.partial(first_coarse_kernel, cap, stride),
        [],
        [arrived, coarse_inverse[0, 0]],
        [shaped(slots, slots, dtype=BF16), shaped(slots, slots, dtype=BF16), slot_shape],
        20 * slots * slots * columns,
    )
    returned = shift(answer, cap)
    half, tiles, energy = call(
        lift_kernel,
        [peers],
        [lift_basis, returned, local, residual],
        [vector_shape, tiles_shape, sum_shape],
        thin,
    )
    incoming = exchange(tiles)
    first, half, tiles, gram_first = call(
        operate_kernel,
        [peers, stiffness],
        [half, incoming, schur_ref],
        [vector_shape, vector_shape, tiles_shape, sum_shape],
        big,
    )
    incoming = exchange(tiles)
    image, outgoing = call(
        residual_kernel, [peers], [half, incoming, slot_basis], [vector_shape, slot_shape], thin
    )
    arrived = shift(outgoing, cap)
    local = call(local_kernel, [], [inverse_local, image], [vector_shape], big)
    answer = call(coarse_kernel, [], [high, low, arrived], [slot_shape], 6 * slots * slots * columns)
    returned = shift(answer, cap)
    half, tiles, gram_mixed = call(
        lift_kernel,
        [peers],
        [lift_basis, returned, local, image],
        [vector_shape, tiles_shape, sum_shape],
        thin,
    )
    incoming = exchange(tiles)
    second, sums = call(
        last_kernel,
        [peers, stiffness],
        [half, incoming, schur_ref, energy, gram_first, gram_mixed],
        [vector_shape, shaped(cores * members, 4, columns)],
        big,
    )
    sums = call(regroup_kernel, [], [gather(sums, layers)], [shaped(chips, 4, columns)])
    sums = gather(sums, lines)
    solution = call(combine_kernel, [], [sums, first, second], [vector_shape])
    return solution.reshape(1, 1, rows_total, columns)


def solution(mesh):
    return jax.shard_map(
        body,
        mesh=mesh,
        in_specs=(
            P("sub", "dom", None, None),
            P("sub", "dom"),
            P(),
            P("sub", "dom", None, None),
            P("sub", "dom", None, None),
            P("sub", "dom", None, None),
            P("sub", "dom", None, None),
            P("sub", "dom", None),
            P("sub", "dom"),
            P("sub", "dom", None, None),
        ),
        out_specs=P("sub", "dom", None, None),
        check_vma=False,
    )
```

time: 336 us -> 304 us (0.905)
  blocking collectives: 120 us -> 155 us
  starting transfers between devices: 58.7 us -> 27.7 us
  waiting for transfers between devices: 101 us -> 81.2 us
  other arithmetic: 12.7 us -> 0.29 us
  Pallas kernels: 0 us -> 12.2 us
  matrix products: 10.2 us -> 1.3 us
  local copies, waits for them, and re-layouts: 30.4 us -> 23.8 us
    all_to_all x5, blocking collectives: 120 us -> 155 us  [the longest x2 96.6 us: shift(): lax.all_to_all(grouped, 'sub', 0, 0, tiled=True)]
    all_to_all x5, starting transfers between devices: 58.7 us -> 27.7 us  [the longest x3 16.2 us: exchange(): return lax.all_to_all(tiles, 'dom', 0, 0, tiled=True)]
    all_to_all x5, waiting for transfers between devices: 101 us -> 81.2 us  [the longest x2 44.8 us: shift(): lax.all_to_all(grouped, 'sub', 0, 0, tiled=True)]
    unnamed x23 -> x66, local copies, waits for them, and re-layouts: 2.79 us -> 20.2 us
    gather x8 -> x0, local copies, waits for them, and re-layouts: 14.8 us -> none  [the longest x4 7.54 us: assemble(): incoming = lax.all_to_all(tiles[slot_source], 'dom', 0, 0, tiled=True)]
    pallas_call x0 -> x13, Pallas kernels: none -> 12.2 us  [call(): pl.pallas_call(kernel, out_shape=outputs[0] if single else tuple(outputs)...]
    dot_general x13 -> x2, matrix products: 10.2 us -> 1.3 us  [chosen(): lax.dot_general(*pair, across, preferred_element_type=F32).astype(BF16)]
    reshape x8 -> x1, local copies, waits for them, and re-layouts: 8.66 us -> 0.13 us  [body(): labels.reshape(groups, 1, cap)]
where the time goes in v2:
time: 304 us; the launch traced here: 303 us
  blocking collectives  155 us (51%)
  waiting for transfers between devices  81.2 us (27%)
  starting transfers between devices  27.7 us (9%)
  local copies, waits for them, and re-layouts  23.8 us (8%)
  Pallas kernels  12.2 us (4%)
    all_to_all x2, blocking collectives, shift(): lax.all_to_all(grouped, 'sub', 0, 0, tiled=True)  96.6 us
    all_to_all x2, waiting for transfers between devices, shift(): lax.all_to_all(grouped, 'sub', 0, 0, tiled=True)  44.8 us
    all_to_all x2, blocking collectives, gather(): lax.all_to_all(values, ('sub', 'dom'), 0, 0, tiled=True, axis_index_group...  39.7 us
    all_to_all x3, waiting for transfers between devices, exchange(): return lax.all_to_all(tiles, 'dom', 0, 0, tiled=True)  36.4 us
    unnamed x66, local copies, waits for them, and re-layouts  20.2 us
    all_to_all x1, blocking collectives, exchange(): return lax.all_to_all(tiles, 'dom', 0, 0, tiled=True)  18.2 us
    all_to_all x3, starting transfers between devices, exchange(): return lax.all_to_all(tiles, 'dom', 0, 0, tiled=True)  16.2 us
    pallas_call x13, Pallas kernels, call(): pl.pallas_call(kernel, out_shape=outputs[0] if single else tuple(outputs)...  12.2 us
  transfers between devices with their start and end apart: 5, of which 5 were waited for; matrix products, arithmetic and copies ran while one was open for 2% of the time, Pallas kernels for 0%

profile of v2, /device:TPU:1, one launch (start us, length us, event | category | flops | bytes accessed | tf_op | source)
XLA Modules:
  0.0 302.6 jit_solution(9986943892445234770)
XLA Ops:
  0.0 1.1 copy-done.6
  1.8 1.6 shard_map.100
  3.4 7.6 %all-to-all-start = ((f32[16,128,128]{2,1,0:T(8,128)}), f32[16,128,128]{2,1,0:T(8,128)S(1)}, u32[]{:S(2)}, u32[]{:S(2)}) async-start(f32[16,128,128]{2,1,0:T(8,128)} %shard_map.100), calls=%async_computation | async-start | bytes 2097152 | tf_op jit(solution)/shard_map/all_to_all | solution.py:205
  13.9 1.0 convolution_convert_fusion.basis_ref
  14.9 8.3 %all-to-all-done.incoming_ref = f32[16,128,128]{2,1,0:T(8,128)S(1)} async-done(((f32[16,128,128]{2,1,0:T(8,128)}), f32[16,128,128]{2,1,0:T(8,128)S(1)}, u32[]{:S(2)}, u32[]{:S(2)}) %all-to-all-start) | async-done | bytes 1048608 | tf_op jit(solution)/shard_map/all_to_all | solution.py:205
  23.2 1.0 copy-done.7
  24.3 1.0 copy-done.18
  26.9 63.1 %all_to_all.50 = f32[64,1,384]{2,1,0:T(1,128)S(1)} all-to-all(f32[64,1,384]{2,1,0:T(1,128)S(1)} %bitcast.35), channel_id=1, replica_groups=mesh['sub'=64,'dom'=16] {'sub'}, dimensions={0} | all-to-all | bytes 196608 | tf_op jit(solution)/shard_map/all_to_all | solution.py:209
  90.0 1.3 shard_map.102
  91.3 5.8 %all-to-all-start.2 = ((f32[64,1,256]{2,1,0:T(1,128)}), f32[64,1,256]{2,1,0:T(1,128)S(1)}, u32[]{:S(2)}, u32[]{:S(2)}) async-start(f32[64,1,256]{2,1,0:T(1,128)} %bitcast.10), calls=%async_computation.2 | async-start | bytes 131072 | tf_op jit(solution)/shard_map/all_to_all | solution.py:209
  97.4 1.1 copy-done.9
  100.0 22.2 %all-to-all-done.2 = f32[64,1,256]{2,1,0:T(1,128)S(1)} async-done(((f32[64,1,256]{2,1,0:T(1,128)}), f32[64,1,256]{2,1,0:T(1,128)S(1)}, u32[]{:S(2)}, u32[]{:S(2)}) %all-to-all-start.2) | async-done | bytes 65568 | tf_op jit(solution)/shard_map/all_to_all | solution.py:209
  122.2 1.0 copy-done.17
  126.0 3.7 %all-to-all-start.3 = ((f32[16,128,128]{2,1,0:T(8,128)}), f32[16,128,128]{2,1,0:T(8,128)S(1)}, u32[]{:S(2)}, u32[]{:S(2)}) async-start(f32[16,128,128]{2,1,0:T(8,128)} %copy-done.20), calls=%async_computation.3 | async-start | bytes 2097152 | tf_op jit(solution)/shard_map/all_to_all | solution.py:205
  130.3 14.6 %all-to-all-done.3.incoming_ref = f32[16,128,128]{2,1,0:T(8,128)S(1)} async-done(((f32[16,128,128]{2,1,0:T(8,128)}), f32[16,128,128]{2,1,0:T(8,128)S(1)}, u32[]{:S(2)}, u32[]{:S(2)}) %all-to-all-start.3) | async-done | bytes 1048608 | tf_op jit(solution)/shard_map/all_to_all | solution.py:205
  144.9 1.6 copy-done.2
  146.5 1.0 copy-done.27
  147.5 1.3 shard_map.105
  148.8 1.0 copy-done.21
  151.4 5.0 %all-to-all-start.4 = ((f32[16,128,128]{2,1,0:T(8,128)}), f32[16,128,128]{2,1,0:T(8,128)S(1)}, u32[]{:S(2)}, u32[]{:S(2)}) async-start(f32[16,128,128]{2,1,0:T(8,128)} %copy-done.21), calls=%async_computation.4 | async-start | bytes 2097152 | tf_op jit(solution)/shard_map/all_to_all | solution.py:205
  156.4 1.8 copy.28.basis_ref
  158.2 13.5 %all-to-all-done.4.incoming_ref = f32[16,128,128]{2,1,0:T(8,128)S(1)} async-done(((f32[16,128,128]{2,1,0:T(8,128)}), f32[16,128,128]{2,1,0:T(8,128)S(1)}, u32[]{:S(2)}, u32[]{:S(2)}) %all-to-all-start.4) | async-done | bytes 1048608 | tf_op jit(solution)/shard_map/all_to_all | solution.py:205
  172.6 1.0 copy-done.25
  175.3 33.5 %all_to_all.51 = f32[64,1,256]{2,1,0:T(1,128)S(1)} all-to-all(f32[64,1,256]{2,1,0:T(1,128)S(1)} %bitcast.37), channel_id=1, replica_groups=mesh['sub'=64,'dom'=16] {'sub'}, dimensions={0} | all-to-all | bytes 131072 | tf_op jit(solution)/shard_map/all_to_all | solution.py:209
  209.6 5.7 %all-to-all-start.6 = ((f32[64,1,256]{2,1,0:T(1,128)}), f32[64,1,256]{2,1,0:T(1,128)S(1)}, u32[]{:S(2)}, u32[]{:S(2)}) async-start(f32[64,1,256]{2,1,0:T(1,128)} %bitcast.15), calls=%async_computation.6 | async-start | bytes 131072 | tf_op jit(solution)/shard_map/all_to_all | solution.py:209
  215.3 1.0 copy-done.12
  217.8 22.6 %all-to-all-done.6 = f32[64,1,256]{2,1,0:T(1,128)S(1)} async-done(((f32[64,1,256]{2,1,0:T(1,128)}), f32[64,1,256]{2,1,0:T(1,128)S(1)}, u32[]{:S(2)}, u32[]{:S(2)}) %all-to-all-start.6) | async-done | bytes 65568 | tf_op jit(solution)/shard_map/all_to_all | solution.py:209
  240.4 1.0 copy-done.15
  242.4 18.2 %all_to_all.52.incoming_ref = f32[16,128,128]{2,1,0:T(8,128)S(1)} all-to-all(f32[16,128,128]{2,1,0:T(8,128)S(1)} %get-tuple-element.36), channel_id=1, replica_groups=mesh['sub'=64,'dom'=16] {'dom'}, dimensions={0} | all-to-all | bytes 2097152 | tf_op jit(solution)/shard_map/all_to_all | solution.py:205
  260.6 1.3 shard_map.110
  261.9 12.6 %all_to_all.53.sums_ref = f32[32,4,128]{2,1,0:T(4,128)S(1)} all-to-all(f32[32,4,128]{2,1,0:T(4,128)S(1)} %get-tuple-element.40), channel_id=1, replica_groups={{0,1,2,3,4,5,6,7,8,9,10,11,12,13,14,15,16,17,18,19,20,21,22,23,24,25,26..., dimensions={0} | all-to-all | bytes 131072 | tf_op jit(solution)/shard_map/all_to_all | solution.py:220
  274.5 27.2 %all_to_all.54.sums_ref = f32[32,4,128]{2,1,0:T(4,128)S(1)} all-to-all(f32[32,4,128]{2,1,0:T(4,128)S(1)} %shard_map.111), channel_id=1, replica_groups={{0,32,64,96,128,160,192,224,256,288,320,352,384,416,448,480,512,544,576..., dimensions={0} | all-to-all | bytes 131072 | tf_op jit(solution)/shard_map/all_to_all | solution.py:220
  (72 shorter events, 17.3 us)
Async XLA Ops:
  0.0 13.9 %copy-start = (bf16[1,1,1024,96]{2,3,1,0:T(8,128)(2,1)S(1)}, bf16[1,1,1024,96]{2,3,1,0:T(8,128)(2,1)}, u32[]{:S(2)}) copy-start(bf16[1,1,1024,96]{2,3,1,0:T(8,128)(2,1)} %param.14) | copy-start | bytes 589828
  0.0 11.7 %copy-start.31 = (s32[1,1,96,1]{2,3,1,0:T(1,128)S(1)}, s32[1,1,96,1]{2,3,1,0:T(1,128)}, u32[]{:S(2)}) copy-start(s32[1,1,96,1]{2,3,1,0:T(1,128)} %param.16) | copy-start | bytes 1156
  0.0 11.9 %copy-start.32 = (s32[1,1,96]{2,1,0:T(1,128)S(1)}, s32[1,1,96]{2,1,0:T(1,128)}, u32[]{:S(2)}) copy-start(s32[1,1,96]{2,1,0:T(1,128)} %param.17) | copy-start | bytes 1156
  0.0 1.1 copy-start.6
  1.8 21.4 %copy-start.29 = (s32[1,1,2,8]{3,2,1,0:T(2,128)S(1)}, s32[1,1,2,8]{3,2,1,0:T(2,128)}, u32[]{:S(2)}) copy-start(s32[1,1,2,8]{3,2,1,0:T(2,128)} %param.15) | copy-start | bytes 196
  3.4 19.8 %all-to-all-start = ((f32[16,128,128]{2,1,0:T(8,128)}), f32[16,128,128]{2,1,0:T(8,128)S(1)}, u32[]{:S(2)}, u32[]{:S(2)}) async-start(f32[16,128,128]{2,1,0:T(8,128)} %shard_map.100), calls=%async_computation | async-start | bytes 2097152 | tf_op jit(solution)/shard_map/all_to_all | solution.py:205
  11.0 79.0 %copy-start.30 = (f32[1,1,64,64]{3,2,1,0:T(8,128)S(1)}, f32[1,1,64,64]{3,2,1,0:T(8,128)}, u32[]{:S(2)}) copy-start(f32[1,1,64,64]{3,2,1,0:T(8,128)} %param.19) | copy-start | bytes 49156
  12.1 85.2 %copy-start.1 = (bf16[1,1,1024,1024]{3,2,1,0:T(8,128)(2,1)S(1)}, bf16[1,1,1024,1024]{3,2,1,0:T(8,128)(2,1)}, u32[]{:S(2)}) copy-start(bf16[1,1,1024,1024]{3,2,1,0:T(8,128)(2,1)} %param.13) | copy-start | bytes 6291460
  23.2 1.0 copy-start.7
  24.3 1.0 copy-start.18
  26.1 0.8 copy-start.8
  26.9 95.3 %copy-start.10 = (f32[1024,128]{1,0:T(8,128)S(1)}, f32[1024,128]{1,0:T(8,128)}, u32[]{:S(2)}) copy-start(f32[1024,128]{1,0:T(8,128)} %copy-done.8) | copy-start | bytes 1572868
  91.3 30.9 %all-to-all-start.2 = ((f32[64,1,256]{2,1,0:T(1,128)}), f32[64,1,256]{2,1,0:T(1,128)S(1)}, u32[]{:S(2)}, u32[]{:S(2)}) async-start(f32[64,1,256]{2,1,0:T(1,128)} %bitcast.10), calls=%async_computation.2 | async-start | bytes 131072 | tf_op jit(solution)/shard_map/all_to_all | solution.py:209
  97.4 26.8 %copy-start.4 = (bf16[128,1024]{0,1:T(8,128)(2,1)}, bf16[128,1024]{0,1:T(8,128)(2,1)S(1)}, u32[]{:S(2)}) copy-start(bf16[128,1024]{0,1:T(8,128)(2,1)S(1)} %convolution_convert_fusion.1) | copy-start | bytes 786436
  97.4 1.1 copy-start.9
  122.2 1.0 copy-start.17
  124.2 1.0 copy-start.20
  126.0 18.9 %all-to-all-start.3 = ((f32[16,128,128]{2,1,0:T(8,128)}), f32[16,128,128]{2,1,0:T(8,128)S(1)}, u32[]{:S(2)}, u32[]{:S(2)}) async-start(f32[16,128,128]{2,1,0:T(8,128)} %copy-done.20), calls=%async_computation.3 | async-start | bytes 2097152 | tf_op jit(solution)/shard_map/all_to_all | solution.py:205
  144.9 1.6 copy-start.2
  146.5 1.0 copy-start.27
  148.8 1.0 copy-start.21
  149.8 0.8 copy-start.22
  151.4 20.3 %all-to-all-start.4 = ((f32[16,128,128]{2,1,0:T(8,128)}), f32[16,128,128]{2,1,0:T(8,128)S(1)}, u32[]{:S(2)}, u32[]{:S(2)}) async-start(f32[16,128,128]{2,1,0:T(8,128)} %copy-done.21), calls=%async_computation.4 | async-start | bytes 2097152 | tf_op jit(solution)/shard_map/all_to_all | solution.py:205
  171.6 1.0 copy-start.19
  172.6 1.0 copy-start.25
  175.3 65.1 %copy-start.5 = (bf16[128,1024]{0,1:T(8,128)(2,1)S(1)}, bf16[128,1024]{0,1:T(8,128)(2,1)}, u32[]{:S(2)}) copy-start(bf16[128,1024]{0,1:T(8,128)(2,1)} %copy-done.4) | copy-start | bytes 786436
  209.6 30.8 %all-to-all-start.6 = ((f32[64,1,256]{2,1,0:T(1,128)}), f32[64,1,256]{2,1,0:T(1,128)S(1)}, u32[]{:S(2)}, u32[]{:S(2)}) async-start(f32[64,1,256]{2,1,0:T(1,128)} %bitcast.15), calls=%async_computation.6 | async-start | bytes 131072 | tf_op jit(solution)/shard_map/all_to_all | solution.py:209
  215.2 1.0 copy-start.12
  216.3 24.1 %copy-start.13 = (f32[1024,128]{1,0:T(8,128)S(1)}, f32[1024,128]{1,0:T(8,128)}, u32[]{:S(2)}) copy-start(f32[1024,128]{1,0:T(8,128)} %copy-done.11) | copy-start | bytes 1572868
  217.8 42.8 %copy-start.3 = (bf16[1024,1024]{1,0:T(8,128)(2,1)S(1)}, bf16[1024,1024]{1,0:T(8,128)(2,1)}, u32[]{:S(2)}) copy-start(bf16[1024,1024]{1,0:T(8,128)(2,1)} %schur_ref.3) | copy-start | bytes 6291460
  240.4 1.0 copy-start.15
  260.6 41.1 %copy-start.23 = (f32[1024,128]{1,0:T(8,128)S(1)}, f32[1024,128]{1,0:T(8,128)}, u32[]{:S(2)}) copy-start(f32[1024,128]{1,0:T(8,128)} %copy-done.22) | copy-start | bytes 1572868
  (6 other events, 4.6 us)

commit v3 on v2

--- a/solution.py
+++ b/solution.py
@@ -47,8 +47,54 @@
     return jnp.sum(value, axis=0, keepdims=True)
 
 
-def send_loads_kernel(peers_ref, loads_ref, out_ref):
+def send_loads_kernel(
+    cap,
+    peers_ref,
+    count_ref,
+    stiffness_ref,
+    loads_ref,
+    basis_ref,
+    routes_ref,
+    rows_ref,
+    out_ref,
+    slot_basis_ref,
+    wide_basis_ref,
+    lift_basis_ref,
+    labels_ref,
+    scale_ref,
+):
     spread(peers_ref, loads_ref[...], out_ref)
+    scale_ref[...] = jnp.full_like(scale_ref, stiffness_ref[0, 0])
+    target = routes_ref[...]
+    listed = target.shape[1]
+    first = lax.broadcasted_iota(jnp.int32, (listed, listed), 0)
+    second = lax.broadcasted_iota(jnp.int32, (listed, listed), 1)
+    column = jnp.sum(jnp.where(first == second, target, 0), axis=1, keepdims=True)
+    ahead = jnp.where(first < second, 1, 0) * jnp.where(column == target, 1, 0)
+    rank = jnp.sum(ahead, axis=0, keepdims=True)
+    live = lax.broadcasted_iota(jnp.int32, target.shape, 1) < count_ref[0, 0]
+    slot = jnp.where(live, target * cap + rank, -1)
+    wide_slot = jnp.where(live, target * (cap + 1) + rank, -1)
+    basis = basis_ref[...]
+
+    def table_of(count, wanted):
+        index = lax.broadcasted_iota(jnp.int32, (count, listed), 0)
+        return jnp.where(index == wanted, 1.0, 0.0).astype(BF16)
+
+    slot_table = table_of(slot_basis_ref.shape[0], slot)
+    slot_basis = dot(slot_table, basis)
+    slot_basis_ref[...] = slot_basis.astype(BF16)
+    lift_basis_ref[...] = jnp.transpose(slot_basis).astype(BF16)
+    wide_basis_ref[...] = dot(table_of(wide_basis_ref.shape[0], wide_slot), basis).astype(BF16)
+    label = jnp.where(live, rows_ref[...] + 1, 0)
+    lane = lax.broadcasted_iota(jnp.int32, labels_ref.shape, 1)
+    index = lax.broadcasted_iota(jnp.int32, (labels_ref.shape[0], listed), 0)
+    labels = jnp.zeros(labels_ref.shape, F32)
+    for i in range(cap):
+        wanted = jnp.where(rank == i, target * (cap + 1) + cap, -1)
+        found = jnp.sum(jnp.where(index == wanted, label, 0), axis=1, keepdims=True)
+        labels = jnp.where(lane == i, found.astype(F32), labels)
+    labels_ref[...] = labels
 
 
 def first_residual_kernel(peers_ref, loads_ref, incoming_ref, basis_ref, labels_ref, residual_ref, out_ref):
@@ -59,10 +105,6 @@
 def residual_kernel(peers_ref, half_ref, incoming_ref, basis_ref, residual_ref, out_ref):
     mirrored(peers_ref, half_ref, incoming_ref, residual_ref)
     out_ref[...] = product(basis_ref[...], 0.5 * residual_ref[...])
-
-
-def local_kernel(inverse_ref, residual_ref, out_ref):
-    out_ref[...] = 0.25 * product(inverse_ref[...], residual_ref[...])
 
 
 def split_product(high, low, value):
@@ -108,28 +150,42 @@
     out_ref[...] = split_product(high_ref[...], low_ref[...], values_ref[...])
 
 
-def lift_kernel(peers_ref, basis_ref, returned_ref, local_ref, residual_ref, half_ref, out_ref, sum_ref):
-    half = local_ref[...] + product(basis_ref[...], returned_ref[...])
+def lift_kernel(
+    peers_ref, inverse_ref, basis_ref, returned_ref, residual_ref, half_ref, out_ref, sum_ref
+):
+    residual = residual_ref[...]
+    half = 0.25 * product(inverse_ref[...], residual) + product(basis_ref[...], returned_ref[...])
     half_ref[...] = half
     spread(peers_ref, half, out_ref)
-    sum_ref[...] = column_sum(residual_ref[...] * half)
-
-
-def operate_kernel(peers_ref, stiffness_ref, half_ref, incoming_ref, schur_ref, vector_ref, image_ref, out_ref, sum_ref):
+    sum_ref[...] = column_sum(residual * half)
+
+
+def operate_kernel(
+    peers_ref, half_ref, incoming_ref, schur_ref, scale_ref, vector_ref, image_ref, out_ref, sum_ref
+):
     mirrored(peers_ref, half_ref, incoming_ref, vector_ref)
     vector = vector_ref[...]
-    image = stiffness_ref[0, 0] * product(schur_ref[...], vector)
+    image = scale_ref[...] * product(schur_ref[...], vector)
     image_ref[...] = image
     spread(peers_ref, image, out_ref)
     sum_ref[...] = column_sum(vector * image)
 
 
 def last_kernel(
-    peers_ref, stiffness_ref, half_ref, incoming_ref, schur_ref, energy_ref, first_ref, mixed_ref, vector_ref, out_ref
+    peers_ref,
+    half_ref,
+    incoming_ref,
+    schur_ref,
+    scale_ref,
+    energy_ref,
+    first_ref,
+    mixed_ref,
+    vector_ref,
+    out_ref,
 ):
     mirrored(peers_ref, half_ref, incoming_ref, vector_ref)
     vector = vector_ref[...]
-    second = stiffness_ref[0, 0] * column_sum(vector * product(schur_ref[...], vector))
+    second = scale_ref[...] * column_sum(vector * product(schur_ref[...], vector))
     sums = jnp.concatenate([energy_ref[...], first_ref[...], mixed_ref[...], second], axis=0)
     out_ref[...] = jnp.broadcast_to(sums[None], out_ref.shape)
 
@@ -187,7 +243,6 @@
     cap = max(2, (primal_max + groups - 1) // groups)
     stride = cap + 1
     slots = groups * cap
-    stiffness = coefficient
     load_tiles = loads[0, 0]
     inverse_local = schur_inverse[0, 0]
 
@@ -219,33 +274,21 @@
     def gather(values, sets):
         return lax.all_to_all(values, ("sub", "dom"), 0, 0, tiled=True, axis_index_groups=sets)
 
-    incoming = exchange(call(send_loads_kernel, [peers], [load_tiles], [tiles_shape]))
-
-    primal_pos = jnp.arange(primal_max, dtype=jnp.int32)
-    live = primal_pos < primal_count[0, 0]
-    target = routes[0, 0, :, 0]
-    ahead = (target[None, :] == target[:, None]) & (primal_pos[None, :] < primal_pos[:, None])
-    rank = jnp.sum(ahead.astype(jnp.int32), axis=1)
-    basis = coarse_basis[0, 0]
-
-    def placed(per_group):
-        wanted = jnp.where(live, target * per_group + rank, -1)
-        return jnp.arange(groups * per_group, dtype=jnp.int32)[:, None] == wanted[None, :]
-
-    def chosen(per_group, basis_first):
-        table = placed(per_group).astype(BF16)
-        pair = (basis, table) if basis_first else (table, basis)
-        across = (((1,), (1,)), ((), ()))
-        return lax.dot_general(*pair, across, preferred_element_type=F32).astype(BF16)
-
-    row_labels = jnp.where(live, coarse_rows[0, 0] + 1, 0)
-    labels = jnp.sum(jnp.where(placed(cap), row_labels[None, :], 0), axis=1)
-    labels = jnp.pad(labels.reshape(groups, 1, cap), ((0, 0), (cap, stride - cap - 1), (0, columns - cap)))
-    labels = labels.reshape(groups * stride, columns).astype(F32)
-    lift_basis = chosen(cap, True)
-    slot_basis = chosen(cap, False)
-    wide_basis = chosen(stride, False)
-
+    outgoing, slot_basis, wide_basis, lift_basis, labels, scale = call(
+        functools.partial(send_loads_kernel, cap),
+        [peers, primal_count, coefficient],
+        [load_tiles, coarse_basis[0, 0].T, routes.reshape(1, primal_max), coarse_rows[0]],
+        [
+            tiles_shape,
+            shaped(slots, rows_total, dtype=BF16),
+            shaped(groups * stride, rows_total, dtype=BF16),
+            shaped(rows_total, slots, dtype=BF16),
+            shaped(groups * stride, columns),
+            sum_shape,
+        ],
+        thin,
+    )
+    incoming = exchange(outgoing)
     residual, outgoing = call(
         first_residual_kernel,
         [peers],
@@ -254,7 +297,6 @@
         2 * thin,
     )
     arrived = shift(outgoing, stride)
-    local = call(local_kernel, [], [inverse_local, residual], [vector_shape], big)
     high, low, answer = call(
         functools.partial(first_coarse_kernel, cap, stride),
         [],
@@ -266,15 +308,15 @@
     half, tiles, energy = call(
         lift_kernel,
         [peers],
-        [lift_basis, returned, local, residual],
+        [inverse_local, lift_basis, returned, residual],
         [vector_shape, tiles_shape, sum_shape],
-        thin,
+        big + thin,
     )
     incoming = exchange(tiles)
     first, half, tiles, gram_first = call(
         operate_kernel,
-        [peers, stiffness],
-        [half, incoming, schur_ref],
+        [peers],
+        [half, incoming, schur_ref, scale],
         [vector_shape, vector_shape, tiles_shape, sum_shape],
         big,
     )
@@ -283,21 +325,20 @@
         residual_kernel, [peers], [half, incoming, slot_basis], [vector_shape, slot_shape], thin
     )
     arrived = shift(outgoing, cap)
-    local = call(local_kernel, [], [inverse_local, image], [vector_shape], big)
     answer = call(coarse_kernel, [], [high, low, arrived], [slot_shape], 6 * slots * slots * columns)
     returned = shift(answer, cap)
     half, tiles, gram_mixed = call(
         lift_kernel,
         [peers],
-        [lift_basis, returned, local, image],
+        [inverse_local, lift_basis, returned, image],
         [vector_shape, tiles_shape, sum_shape],
-        thin,
+        big + thin,
     )
     incoming = exchange(tiles)
     second, sums = call(
         last_kernel,
-        [peers, stiffness],
-        [half, incoming, schur_ref, energy, gram_first, gram_mixed],
+        [peers],
+        [half, incoming, schur_ref, scale, energy, gram_first, gram_mixed],
         [vector_shape, shaped(cores * members, 4, columns)],
         big,
     )

time: 304 us -> 286 us (0.941)
  blocking collectives: 155 us -> 270 us
  waiting for transfers between devices: 81.2 us -> 0 us
  starting transfers between devices: 27.7 us -> 0 us
  local copies, waits for them, and re-layouts: 23.8 us -> 3.97 us
    all_to_all x5 -> x0, waiting for transfers between devices: 81.2 us -> none  [the longest x2 44.8 us: shift(): lax.all_to_all(grouped, 'sub', 0, 0, tiled=True)]
    all_to_all x2 -> x4, blocking collectives: 96.6 us -> 157 us  [shift(): lax.all_to_all(grouped, 'sub', 0, 0, tiled=True)]
    all_to_all x1 -> x4, blocking collectives: 18.2 us -> 73.5 us  [exchange(): return lax.all_to_all(tiles, 'dom', 0, 0, tiled=True)]
    all_to_all x5 -> x0, starting transfers between devices: 27.7 us -> none  [the longest x3 16.2 us: exchange(): return lax.all_to_all(tiles, 'dom', 0, 0, tiled=True)]
    unnamed x66 -> x18, local copies, waits for them, and re-layouts: 20.2 us -> 3.97 us
    convert_element_type x3 -> x0, local copies, waits for them, and re-layouts: 3.46 us -> none  [the longest x1 1.78 us: chosen(): lax.dot_general(*pair, across, preferred_element_type=F32).astype(BF16)]
    pallas_call x13 -> x11, Pallas kernels: 12.2 us -> 10.1 us  [call(): pl.pallas_call(kernel, out_shape=outputs[0] if single else tuple(outputs)...]
  transfers between devices with their start and end apart: 5 -> 0, of which waited for: 5 -> 0; matrix products, arithmetic and copies ran while one was open for 2% -> 0% of each run, Pallas kernels for 0% -> 0%
where the time goes in v3:
time: 286 us; the launch traced here: 285 us
  blocking collectives  270 us (94%)
  Pallas kernels  10.1 us (4%)
  local copies, waits for them, and re-layouts  3.97 us (1%)
    all_to_all x4, blocking collectives, shift(): lax.all_to_all(grouped, 'sub', 0, 0, tiled=True)  157 us
    all_to_all x4, blocking collectives, exchange(): return lax.all_to_all(tiles, 'dom', 0, 0, tiled=True)  73.5 us
    all_to_all x2, blocking collectives, gather(): lax.all_to_all(values, ('sub', 'dom'), 0, 0, tiled=True, axis_index_group...  39.8 us
    pallas_call x11, Pallas kernels, call(): pl.pallas_call(kernel, out_shape=outputs[0] if single else tuple(outputs)...  10.1 us

profile of v3, /device:TPU:1, one launch (start us, length us, event | category | flops | bytes accessed | tf_op | source)
XLA Modules:
  0.0 285.4 jit_solution(15462610485273478550)
XLA Ops:
  1.3 0.0 copy-start.2
  1.3 1.0 copy-done.2
  2.3 0.9 copy-done.3
  3.3 0.7 copy-done.4
  3.9 0.7 copy-done.6
  4.6 0.7 copy-done.7
  5.3 1.0 shard_map.100
  6.3 0.0 copy-start.8
  6.3 0.0 copy-start
  6.3 0.0 copy-start.5
  6.3 19.4 %all_to_all.50.incoming_ref = f32[16,128,128]{2,1,0:T(8,128)S(1)} all-to-all(f32[16,128,128]{2,1,0:T(8,128)S(1)} %get-tuple-element.31), channel_id=1, replica_groups=mesh['sub'=64,'dom'=16] {'dom'}, dimensions={0} | all-to-all | bytes 2097152 | tf_op jit(solution)/shard_map/all_to_all | solution.py:260
  25.7 0.8 shard_map.101
  26.5 62.9 %all_to_all.51 = f32[64,1,384]{2,1,0:T(1,128)S(1)} all-to-all(f32[64,1,384]{2,1,0:T(1,128)S(1)} %bitcast.27), channel_id=1, replica_groups=mesh['sub'=64,'dom'=16] {'sub'}, dimensions={0} | all-to-all | bytes 196608 | tf_op jit(solution)/shard_map/all_to_all | solution.py:264
  89.4 0.0 copy-done.8
  89.4 0.6 shard_map.102
  90.0 30.5 %all_to_all.52 = f32[64,1,256]{2,1,0:T(1,128)S(1)} all-to-all(f32[64,1,256]{2,1,0:T(1,128)S(1)} %bitcast.30), channel_id=1, replica_groups=mesh['sub'=64,'dom'=16] {'sub'}, dimensions={0} | all-to-all | bytes 131072 | tf_op jit(solution)/shard_map/all_to_all | solution.py:264
  120.5 0.0 copy-done
  120.5 1.5 shard_map.103
  122.0 18.3 %all_to_all.53.incoming_ref = f32[16,128,128]{2,1,0:T(8,128)S(1)} all-to-all(f32[16,128,128]{2,1,0:T(8,128)S(1)} %get-tuple-element.40), channel_id=1, replica_groups=mesh['sub'=64,'dom'=16] {'dom'}, dimensions={0} | all-to-all | bytes 2097152 | tf_op jit(solution)/shard_map/all_to_all | solution.py:260
  140.3 0.0 copy-done.1
  140.3 1.3 shard_map.104
  141.6 17.5 %all_to_all.54.incoming_ref = f32[16,128,128]{2,1,0:T(8,128)S(1)} all-to-all(f32[16,128,128]{2,1,0:T(8,128)S(1)} %get-tuple-element.43), channel_id=1, replica_groups=mesh['sub'=64,'dom'=16] {'dom'}, dimensions={0} | all-to-all | bytes 2097152 | tf_op jit(solution)/shard_map/all_to_all | solution.py:260
  159.1 0.8 shard_map.105
  159.9 33.0 %all_to_all.55 = f32[64,1,256]{2,1,0:T(1,128)S(1)} all-to-all(f32[64,1,256]{2,1,0:T(1,128)S(1)} %bitcast.29), channel_id=1, replica_groups=mesh['sub'=64,'dom'=16] {'sub'}, dimensions={0} | all-to-all | bytes 131072 | tf_op jit(solution)/shard_map/all_to_all | solution.py:264
  193.0 0.2 shard_map.106
  193.1 30.4 %all_to_all.56 = f32[64,1,256]{2,1,0:T(1,128)S(1)} all-to-all(f32[64,1,256]{2,1,0:T(1,128)S(1)} %bitcast.25), channel_id=1, replica_groups=mesh['sub'=64,'dom'=16] {'sub'}, dimensions={0} | all-to-all | bytes 131072 | tf_op jit(solution)/shard_map/all_to_all | solution.py:264
  223.5 1.5 shard_map.107
  225.0 18.3 %all_to_all.57.incoming_ref = f32[16,128,128]{2,1,0:T(8,128)S(1)} all-to-all(f32[16,128,128]{2,1,0:T(8,128)S(1)} %get-tuple-element.48), channel_id=1, replica_groups=mesh['sub'=64,'dom'=16] {'dom'}, dimensions={0} | all-to-all | bytes 2097152 | tf_op jit(solution)/shard_map/all_to_all | solution.py:260
  243.3 1.3 shard_map.108
  244.6 12.6 %all_to_all.58.sums_ref = f32[32,4,128]{2,1,0:T(4,128)S(1)} all-to-all(f32[32,4,128]{2,1,0:T(4,128)S(1)} %get-tuple-element.52), channel_id=1, replica_groups={{0,1,2,3,4,5,6,7,8,9,10,11,12,13,14,15,16,17,18,19,20,21,22,23,24,25,26..., dimensions={0} | all-to-all | bytes 131072 | tf_op jit(solution)/shard_map/all_to_all | solution.py:275
  257.3 27.3 %all_to_all.59.sums_ref = f32[32,4,128]{2,1,0:T(4,128)S(1)} all-to-all(f32[32,4,128]{2,1,0:T(4,128)S(1)} %shard_map.109), channel_id=1, replica_groups={{0,32,64,96,128,160,192,224,256,288,320,352,384,416,448,480,512,544,576..., dimensions={0} | all-to-all | bytes 131072 | tf_op jit(solution)/shard_map/all_to_all | solution.py:275
  284.5 0.9 shard_map.110
  (7 shorter events, 0.1 us)
Async XLA Ops:
  1.3 1.0 copy-start.2
  2.3 0.9 copy-start.3
  3.3 0.7 copy-start.4
  3.9 0.7 copy-start.6
  4.6 0.7 copy-start.7
  6.3 83.1 %copy-start.8 = (f32[1,1,64,64]{3,2,1,0:T(8,128)S(1)}, f32[1,1,64,64]{3,2,1,0:T(8,128)}, u32[]{:S(2)}) copy-start(f32[1,1,64,64]{3,2,1,0:T(8,128)} %param.19) | copy-start | bytes 49156
  6.3 114.2 %copy-start = (bf16[1,1,1024,1024]{3,2,1,0:T(8,128)(2,1)S(1)}, bf16[1,1,1024,1024]{3,2,1,0:T(8,128)(2,1)}, u32[]{:S(2)}) copy-start(bf16[1,1,1024,1024]{3,2,1,0:T(8,128)(2,1)} %param.13) | copy-start | bytes 6291460
  6.3 114.2 %copy-start.5 = (s32[1,1,2,8]{3,2,1,0:T(2,128)S(1)}, s32[1,1,2,8]{3,2,1,0:T(2,128)}, u32[]{:S(2)}) copy-start(s32[1,1,2,8]{3,2,1,0:T(2,128)} %param.15) | copy-start | bytes 196
  120.5 19.8 %copy-start.1 = (bf16[1024,1024]{1,0:T(8,128)(2,1)S(1)}, bf16[1024,1024]{1,0:T(8,128)(2,1)}, u32[]{:S(2)}) copy-start(bf16[1024,1024]{1,0:T(8,128)(2,1)} %schur_ref.3) | copy-start | bytes 6291460

commit v4 on v3

--- a/solution.py
+++ b/solution.py
@@ -1,4 +1,5 @@
 import functools
+import math
 
 import jax
 import jax.numpy as jnp
@@ -29,43 +30,73 @@
     return both[:, :columns] + both[:, columns:]
 
 
+def middle_of_plane(members):
+    side = math.isqrt(members)
+    return side // 2 * side + side // 2
+
+
+def rotated(count, first):
+    return [(first + i) % count for i in range(count)]
+
+
+def place_of(peers_ref, t, members):
+    return lax.rem(peers_ref[0, t] + (members - middle_of_plane(members)), members)
+
+
 def spread(peers_ref, value, out_ref):
-    tile = out_ref.shape[1]
+    members, tile = out_ref.shape[:2]
     out_ref[...] = jnp.zeros_like(out_ref)
     for t in range(value.shape[0] // tile):
-        out_ref[peers_ref[0, t]] = value[t * tile : (t + 1) * tile]
+        out_ref[place_of(peers_ref, t, members)] = value[t * tile : (t + 1) * tile]
 
 
 def mirrored(peers_ref, half_ref, incoming_ref, out_ref):
-    tile = incoming_ref.shape[1]
+    members, tile = incoming_ref.shape[:2]
     for t in range(half_ref.shape[0] // tile):
         rows = slice(t * tile, (t + 1) * tile)
-        out_ref[rows] = half_ref[rows] + incoming_ref[peers_ref[0, t]]
+        out_ref[rows] = half_ref[rows] + incoming_ref[place_of(peers_ref, t, members)]
 
 
 def column_sum(value):
     return jnp.sum(value, axis=0, keepdims=True)
 
 
-def send_loads_kernel(
+def first_kernel(
     cap,
-    peers_ref,
     count_ref,
     stiffness_ref,
-    loads_ref,
-    basis_ref,
-    routes_ref,
-    rows_ref,
+    peers_hbm,
+    routes_hbm,
+    rows_hbm,
+    loads_hbm,
+    basis_hbm,
     out_ref,
     slot_basis_ref,
     wide_basis_ref,
     lift_basis_ref,
     labels_ref,
     scale_ref,
+    peers_ref,
+    routes_ref,
+    rows_ref,
+    loads_ref,
+    basis_ref,
+    semaphores,
 ):
+    sources = (peers_hbm, routes_hbm, rows_hbm, loads_hbm, basis_hbm)
+    targets = (peers_ref, routes_ref, rows_ref, loads_ref, basis_ref)
+    copies = [
+        pltpu.make_async_copy(source, target, semaphores.at[i])
+        for i, (source, target) in enumerate(zip(sources, targets))
+    ]
+    for copy in copies:
+        copy.start()
+    scale_ref[...] = jnp.full_like(scale_ref, stiffness_ref[0, 0])
+    for copy in copies:
+        copy.wait()
     spread(peers_ref, loads_ref[...], out_ref)
-    scale_ref[...] = jnp.full_like(scale_ref, stiffness_ref[0, 0])
-    target = routes_ref[...]
+    groups = slot_basis_ref.shape[0] // cap
+    target = lax.rem(routes_ref[...] + (groups - groups // 2), groups)
     listed = target.shape[1]
     first = lax.broadcasted_iota(jnp.int32, (listed, listed), 0)
     second = lax.broadcasted_iota(jnp.int32, (listed, listed), 1)
@@ -207,15 +238,16 @@
     out_ref[...] = along_first * first_ref[...] - along_second * second_ref[...]
 
 
-def call(kernel, scalars, inputs, outputs, flops=0):
+def call(kernel, scalars, inputs, outputs, flops=0, in_specs=None, scratch_shapes=()):
     moved = sum(x.size * x.dtype.itemsize for x in inputs)
     moved += sum(x.size * x.dtype.itemsize for x in outputs)
     single = len(outputs) == 1
     return pl.pallas_call(
         kernel,
         out_shape=outputs[0] if single else tuple(outputs),
-        in_specs=[SMEM] * len(scalars) + [VMEM] * len(inputs),
+        in_specs=in_specs or [SMEM] * len(scalars) + [VMEM] * len(inputs),
         out_specs=VMEM if single else tuple([VMEM] * len(outputs)),
+        scratch_shapes=scratch_shapes,
         compiler_params=pltpu.CompilerParams(vmem_limit_bytes=20 << 20),
         cost_estimate=pl.CostEstimate(flops=flops, bytes_accessed=moved, transcendentals=0),
     )(*scalars, *inputs)
@@ -256,28 +288,40 @@
     big = 4 * rows_total * rows_total * columns
     thin = 4 * rows_total * slots * columns
 
+    plane = rotated(members, middle_of_plane(members))
+    ring = rotated(groups, groups // 2)
+
     def exchange(tiles):
-        return lax.all_to_all(tiles, "dom", 0, 0, tiled=True)
+        return lax.all_to_all(tiles, "dom", 0, 0, tiled=True, axis_index_groups=[plane])
 
     def shift(values, per_group):
         grouped = values.reshape(groups, 1, per_group * columns)
-        return lax.all_to_all(grouped, "sub", 0, 0, tiled=True).reshape(groups * per_group, columns)
+        moved = lax.all_to_all(grouped, "sub", 0, 0, tiled=True, axis_index_groups=[ring])
+        return moved.reshape(groups * per_group, columns)
 
     cores = 2
     chips = groups // cores
     layers = [
-        [(z * cores + k) * members + d for k in range(cores) for d in range(members)]
-        for z in range(chips)
+        [(z * cores + k) * members + d for k in range(cores) for d in plane]
+        for z in rotated(chips, chips // 2)
     ]
     lines = [list(line) for line in zip(*layers)]
 
     def gather(values, sets):
         return lax.all_to_all(values, ("sub", "dom"), 0, 0, tiled=True, axis_index_groups=sets)
 
+    given = [
+        peers,
+        routes.reshape(1, primal_max),
+        coarse_rows[0],
+        load_tiles,
+        coarse_basis[0, 0].T,
+    ]
+    spaces = [pltpu.SMEM] + [pltpu.VMEM] * 4
     outgoing, slot_basis, wide_basis, lift_basis, labels, scale = call(
-        functools.partial(send_loads_kernel, cap),
-        [peers, primal_count, coefficient],
-        [load_tiles, coarse_basis[0, 0].T, routes.reshape(1, primal_max), coarse_rows[0]],
+        functools.partial(first_kernel, cap),
+        [primal_count, coefficient],
+        [pltpu.with_memory_space_constraint(x, pltpu.HBM) for x in given],
         [
             tiles_shape,
             shaped(slots, rows_total, dtype=BF16),
@@ -287,6 +331,9 @@
             sum_shape,
         ],
         thin,
+        in_specs=[SMEM] * 2 + [pl.BlockSpec(memory_space=pltpu.HBM)] * len(given),
+        scratch_shapes=[space(x.shape, x.dtype) for space, x in zip(spaces, given)]
+        + [pltpu.SemaphoreType.DMA((len(given),))],
     )
     incoming = exchange(outgoing)
     residual, outgoing = call(

time: 286 us -> 266 us (0.930)
  blocking collectives: 270 us -> 254 us
  local copies, waits for them, and re-layouts: 3.97 us -> 0.02 us
    all_to_all x8, blocking collectives: 230 us -> 215 us  [the longest x4 142 us: shift(): lax.all_to_all(grouped, 'sub', 0, 0, tiled=True, axis_index_groups=[ring])]
    unnamed x18 -> x10, local copies, waits for them, and re-layouts: 3.97 us -> 0.02 us
where the time goes in v4:
time: 266 us
  blocking collectives  254 us (95%)
  Pallas kernels  10.8 us (4%)
    all_to_all x4, blocking collectives, shift(): lax.all_to_all(grouped, 'sub', 0, 0, tiled=True, axis_index_groups=[ring])  142 us
    all_to_all x4, blocking collectives, exchange(): lax.all_to_all(tiles, 'dom', 0, 0, tiled=True, axis_index_groups=[plane])  73.1 us
    all_to_all x2, blocking collectives, gather(): lax.all_to_all(values, ('sub', 'dom'), 0, 0, tiled=True, axis_index_group...  38.4 us
    pallas_call x11, Pallas kernels, call(): pl.pallas_call(kernel, out_shape=outputs[0] if single else tuple(outputs)...  10.8 us

profile of v4, /device:TPU:1, one launch (start us, length us, event | category | flops | bytes accessed | tf_op | source)
XLA Modules:
  0.0 265.9 jit_solution(5998051369428624394)
XLA Ops:
  0.0 0.0 copy-start.3
  0.0 0.0 copy-start.2
  1.4 1.7 shard_map.100
  3.1 0.0 copy-start.4
  3.1 0.0 copy-start
  3.1 16.1 %all_to_all.50.incoming_ref = f32[16,128,128]{2,1,0:T(8,128)S(1)} all-to-all(f32[16,128,128]{2,1,0:T(8,128)S(1)} %get-tuple-element.31), channel_id=1, replica_groups={{10,11,12,13,14,15,0,1,2,3,4,5,6,7,8,9},{26,27,28,29,30,31,16,17,18,19,..., dimensions={0} | all-to-all | bytes 2097152 | tf_op jit(solution)/shard_map/all_to_all | solution.py:295
  19.2 0.0 copy-done.3
  19.2 0.0 copy-done.2
  19.3 0.8 shard_map.101
  20.1 51.7 %all_to_all.51 = f32[64,1,384]{2,1,0:T(1,128)S(1)} all-to-all(f32[64,1,384]{2,1,0:T(1,128)S(1)} %bitcast.26), channel_id=1, replica_groups={{512,528,544,560,576,592,608,624,640,656,672,688,704,720,736,752,768,78..., dimensions={0} | all-to-all | bytes 196608 | tf_op jit(solution)/shard_map/all_to_all | solution.py:299
  71.8 0.0 copy-done.4
  71.8 0.6 shard_map.102
  72.4 30.1 %all_to_all.52 = f32[64,1,256]{2,1,0:T(1,128)S(1)} all-to-all(f32[64,1,256]{2,1,0:T(1,128)S(1)} %bitcast.29), channel_id=1, replica_groups={{512,528,544,560,576,592,608,624,640,656,672,688,704,720,736,752,768,78..., dimensions={0} | all-to-all | bytes 131072 | tf_op jit(solution)/shard_map/all_to_all | solution.py:299
  102.5 0.0 copy-done
  102.5 0.0 copy-start.1
  102.5 1.5 shard_map.103
  104.0 19.1 %all_to_all.53.incoming_ref = f32[16,128,128]{2,1,0:T(8,128)S(1)} all-to-all(f32[16,128,128]{2,1,0:T(8,128)S(1)} %get-tuple-element.40), channel_id=1, replica_groups={{10,11,12,13,14,15,0,1,2,3,4,5,6,7,8,9},{26,27,28,29,30,31,16,17,18,19,..., dimensions={0} | all-to-all | bytes 2097152 | tf_op jit(solution)/shard_map/all_to_all | solution.py:295
  123.1 0.0 copy-done.1
  123.1 1.3 shard_map.104
  124.4 18.8 %all_to_all.54.incoming_ref = f32[16,128,128]{2,1,0:T(8,128)S(1)} all-to-all(f32[16,128,128]{2,1,0:T(8,128)S(1)} %get-tuple-element.43), channel_id=1, replica_groups={{10,11,12,13,14,15,0,1,2,3,4,5,6,7,8,9},{26,27,28,29,30,31,16,17,18,19,..., dimensions={0} | all-to-all | bytes 2097152 | tf_op jit(solution)/shard_map/all_to_all | solution.py:295
  143.2 0.8 shard_map.105
  144.0 30.1 %all_to_all.55 = f32[64,1,256]{2,1,0:T(1,128)S(1)} all-to-all(f32[64,1,256]{2,1,0:T(1,128)S(1)} %bitcast.28), channel_id=1, replica_groups={{512,528,544,560,576,592,608,624,640,656,672,688,704,720,736,752,768,78..., dimensions={0} | all-to-all | bytes 131072 | tf_op jit(solution)/shard_map/all_to_all | solution.py:299
  174.2 0.2 shard_map.106
  174.3 30.2 %all_to_all.56 = f32[64,1,256]{2,1,0:T(1,128)S(1)} all-to-all(f32[64,1,256]{2,1,0:T(1,128)S(1)} %bitcast.25), channel_id=1, replica_groups={{512,528,544,560,576,592,608,624,640,656,672,688,704,720,736,752,768,78..., dimensions={0} | all-to-all | bytes 131072 | tf_op jit(solution)/shard_map/all_to_all | solution.py:299
  204.5 1.5 shard_map.107
  206.0 19.1 %all_to_all.57.incoming_ref = f32[16,128,128]{2,1,0:T(8,128)S(1)} all-to-all(f32[16,128,128]{2,1,0:T(8,128)S(1)} %get-tuple-element.48), channel_id=1, replica_groups={{10,11,12,13,14,15,0,1,2,3,4,5,6,7,8,9},{26,27,28,29,30,31,16,17,18,19,..., dimensions={0} | all-to-all | bytes 2097152 | tf_op jit(solution)/shard_map/all_to_all | solution.py:295
  225.2 1.3 shard_map.108
  226.5 10.5 %all_to_all.58.sums_ref = f32[32,4,128]{2,1,0:T(4,128)S(1)} all-to-all(f32[32,4,128]{2,1,0:T(4,128)S(1)} %get-tuple-element.52), channel_id=1, replica_groups={{522,523,524,525,526,527,512,513,514,515,516,517,518,519,520,521,538,53..., dimensions={0} | all-to-all | bytes 131072 | tf_op jit(solution)/shard_map/all_to_all | solution.py:311
  237.0 27.9 %all_to_all.59.sums_ref = f32[32,4,128]{2,1,0:T(4,128)S(1)} all-to-all(f32[32,4,128]{2,1,0:T(4,128)S(1)} %shard_map.109), channel_id=1, replica_groups={{522,554,586,618,650,682,714,746,778,810,842,874,906,938,970,1002,10,42..., dimensions={0} | all-to-all | bytes 131072 | tf_op jit(solution)/shard_map/all_to_all | solution.py:311
  265.0 0.9 shard_map.110
  (1 shorter events, 0.0 us)
Async XLA Ops:
  0.0 19.2 %copy-start.3 = (s32[1,1,2,8]{3,2,1,0:T(2,128)S(1)}, s32[1,1,2,8]{3,2,1,0:T(2,128)}, u32[]{:S(2)}) copy-start(s32[1,1,2,8]{3,2,1,0:T(2,128)} %param.15) | copy-start | bytes 196
  0.0 19.2 %copy-start.2 = (f32[1,1,1024,128]{3,2,1,0:T(8,128)S(1)}, f32[1,1,1024,128]{3,2,1,0:T(8,128)}, u32[]{:S(2)}) copy-start(f32[1,1,1024,128]{3,2,1,0:T(8,128)} %param.10) | copy-start | bytes 1572868
  3.1 68.7 %copy-start.4 = (f32[1,1,64,64]{3,2,1,0:T(8,128)S(1)}, f32[1,1,64,64]{3,2,1,0:T(8,128)}, u32[]{:S(2)}) copy-start(f32[1,1,64,64]{3,2,1,0:T(8,128)} %param.19) | copy-start | bytes 49156
  3.1 99.4 %copy-start = (bf16[1,1,1024,1024]{3,2,1,0:T(8,128)(2,1)S(1)}, bf16[1,1,1024,1024]{3,2,1,0:T(8,128)(2,1)}, u32[]{:S(2)}) copy-start(bf16[1,1,1024,1024]{3,2,1,0:T(8,128)(2,1)} %param.13) | copy-start | bytes 6291460
  102.5 20.6 %copy-start.1 = (bf16[1024,1024]{1,0:T(8,128)(2,1)S(1)}, bf16[1024,1024]{1,0:T(8,128)(2,1)}, u32[]{:S(2)}) copy-start(bf16[1024,1024]{1,0:T(8,128)(2,1)} %schur_ref.3) | copy-start | bytes 6291460

commit v5 on v4

v5 whole, which is shorter than its diff:
```python
import functools
import math

import jax
import jax.numpy as jnp
from jax import lax
from jax.experimental import pallas as pl
from jax.experimental.pallas import tpu as pltpu
from jax.sharding import PartitionSpec as P

F32 = jnp.float32
BF16 = jnp.bfloat16
VMEM = pl.BlockSpec(memory_space=pltpu.VMEM)
SMEM = pl.BlockSpec(memory_space=pltpu.SMEM)


def parts_of(value):
    high = value.astype(BF16)
    low = (value - high.astype(F32)).astype(BF16)
    return high, low


def dot(left, right):
    return jnp.dot(left, right, preferred_element_type=F32)


def product(matrix, value):
    columns = value.shape[1]
    both = dot(matrix, jnp.concatenate(parts_of(value), axis=1))
    return both[:, :columns] + both[:, columns:]


def row_product(value, matrix):
    rows = value.shape[0]
    both = dot(jnp.concatenate(parts_of(value), axis=0), matrix)
    return both[:rows] + both[rows:]


def middle_of_plane(members):
    side = math.isqrt(members)
    return side // 2 * side + side // 2


def rotated(count, first):
    return [(first + i) % count for i in range(count)]


def place_of(peers_ref, t, members):
    return lax.rem(peers_ref[0, t] + (members - middle_of_plane(members)), members)


def each_tile(blocks, tiles):
    return [(p, t) for p in range(blocks) for t in range(tiles)]


def block(ref, p, t, rows, lanes):
    return ref.at[p * rows : (p + 1) * rows, t * lanes : (t + 1) * lanes]


def first_kernel(
    cap,
    count_ref,
    stiffness_ref,
    peers_hbm,
    routes_hbm,
    rows_hbm,
    loads_hbm,
    basis_hbm,
    out_ref,
    slot_basis_ref,
    wide_basis_ref,
    labels_ref,
    peers_ref,
    listed_ref,
    routes_ref,
    rows_ref,
    loads_ref,
    basis_ref,
    about_ref,
    semaphores,
):
    sources = (peers_hbm, peers_hbm, routes_hbm, rows_hbm, loads_hbm, basis_hbm)
    targets = (peers_ref, listed_ref, routes_ref, rows_ref, loads_ref, basis_ref)
    copies = [
        pltpu.make_async_copy(source, target, semaphores.at[i])
        for i, (source, target) in enumerate(zip(sources, targets))
    ]
    for copy in copies:
        copy.start()
    about_ref[...] = jnp.full_like(about_ref, stiffness_ref[0, 0])
    for copy in copies:
        copy.wait()
    tile_count = listed_ref.shape[1]
    tile = loads_ref.shape[0] // tile_count
    members = out_ref.shape[0]
    about_ref[0:1, 0:tile_count] = listed_ref[0:1, :].astype(F32)
    out_ref[:, 0:tile] = jnp.zeros((members, tile, out_ref.shape[2]), F32)
    for m in range(members):
        out_ref[m, tile:] = about_ref[...]
    for t in range(tile_count):
        out_ref[place_of(peers_ref, t, members), 0:tile] = loads_ref[t * tile : (t + 1) * tile]
    groups = slot_basis_ref.shape[0] // cap
    target = lax.rem(routes_ref[...] + (groups - groups // 2), groups)
    listed = target.shape[1]
    first = lax.broadcasted_iota(jnp.int32, (listed, listed), 0)
    second = lax.broadcasted_iota(jnp.int32, (listed, listed), 1)
    column = jnp.sum(jnp.where(first == second, target, 0), axis=1, keepdims=True)
    ahead = jnp.where(first < second, 1, 0) * jnp.where(column == target, 1, 0)
    rank = jnp.sum(ahead, axis=0, keepdims=True)
    live = lax.broadcasted_iota(jnp.int32, target.shape, 1) < count_ref[0, 0]
    slot = jnp.where(live, target * cap + rank, -1)
    wide_slot = jnp.where(live, target * (cap + 1) + rank, -1)
    basis = basis_ref[...]

    def table_of(count, wanted):
        index = lax.broadcasted_iota(jnp.int32, (count, listed), 0)
        return jnp.where(index == wanted, 1.0, 0.0).astype(BF16)

    slot_table = table_of(slot_basis_ref.shape[0], slot)
    slot_basis_ref[...] = dot(slot_table, basis).astype(BF16)
    wide_basis_ref[...] = dot(table_of(wide_basis_ref.shape[0], wide_slot), basis).astype(BF16)
    label = jnp.where(live, rows_ref[...] + 1, 0)
    lane = lax.broadcasted_iota(jnp.int32, labels_ref.shape, 1)
    index = lax.broadcasted_iota(jnp.int32, (labels_ref.shape[0], listed), 0)
    labels = jnp.zeros(labels_ref.shape, F32)
    for i in range(cap):
        wanted = jnp.where(rank == i, target * (cap + 1) + cap, -1)
        found = jnp.sum(jnp.where(index == wanted, label, 0), axis=1, keepdims=True)
        labels = jnp.where(lane == i, found.astype(F32), labels)
    labels_ref[...] = labels


def first_residual_kernel(
    peers_ref,
    loads_ref,
    incoming_ref,
    basis_ref,
    labels_ref,
    residual_ref,
    out_ref,
    listed_ref,
    scale_ref,
    sum_ref,
):
    members = incoming_ref.shape[0]
    columns, rows_total = residual_ref.shape
    tile = rows_total // peers_ref.shape[1]
    share = columns // members
    for t in range(peers_ref.shape[1]):
        rows = slice(t * tile, (t + 1) * tile)
        total = loads_ref[rows] + incoming_ref[place_of(peers_ref, t, members), 0:tile]
        sum_ref[rows] = total
        residual_ref[:, rows] = jnp.transpose(total)
    out_ref[...] = product(basis_ref[...], 0.5 * sum_ref[...]) + labels_ref[...]
    turn = members - middle_of_plane(members)
    for m in range(members):
        listed = incoming_ref[m, tile : tile + 1].astype(jnp.int32)
        listed_ref[m : m + 1] = lax.rem(listed + turn, members)
        stiffness = incoming_ref[m, tile + 1 : tile + 2]
        scale_ref[m * share : (m + 1) * share] = jnp.broadcast_to(stiffness, (share, columns))


def residual_kernel(incoming_ref, basis_ref, residual_ref, out_ref):
    members, tiles, share, tile = incoming_ref.shape
    for p, t in each_tile(members, tiles):
        block(residual_ref, p, t, share, tile)[...] = incoming_ref[p, t]
    columns = residual_ref.shape[0]
    both = lax.dot_general(
        basis_ref[...],
        jnp.concatenate(parts_of(0.5 * residual_ref[...]), axis=0),
        (((1,), (1,)), ((), ())),
        preferred_element_type=F32,
    )
    out_ref[...] = both[:, :columns] + both[:, columns:]


def split_product(high, low, value):
    value_high, value_low = parts_of(value)
    return dot(
        jnp.concatenate([high, high, low], axis=1),
        jnp.concatenate([value_high, value_low, value_high], axis=0),
    )


def first_coarse_kernel(cap, stride, arrived_ref, block_ref, high_ref, low_ref, out_ref):
    slots, columns = out_ref.shape
    coarse_size = block_ref.shape[0]
    received = arrived_ref.shape[0]
    arrived = jnp.concatenate(parts_of(arrived_ref[...]), axis=1)
    slot = lax.broadcasted_iota(jnp.int32, (slots, received), 0)
    row = lax.broadcasted_iota(jnp.int32, (slots, received), 1)
    base = (slot // cap) * stride
    pick_value = (row == base + slot % cap).astype(F32).astype(BF16)
    pick_label = (row == base + cap).astype(F32).astype(BF16)
    values = dot(pick_value, arrived)
    values = values[:, :columns] + values[:, columns:]
    label_rows = dot(pick_label, arrived[:, :columns])
    lane = lax.broadcasted_iota(jnp.int32, (slots, columns), 1)
    own = lax.broadcasted_iota(jnp.int32, (slots, columns), 0) % cap
    labels = jnp.sum(jnp.where(lane == own, label_rows, 0.0), axis=1, keepdims=True)
    ids = lax.broadcasted_iota(jnp.int32, (slots, coarse_size), 1).astype(F32)
    owner = (labels - 1.0 == ids).astype(F32).astype(BF16)
    block_high, block_low = parts_of(block_ref[...])
    across = (((1,), (1,)), ((), ()))

    def composed(part):
        rows = dot(owner, part).astype(BF16)
        return lax.dot_general(rows, owner, across, preferred_element_type=F32).astype(BF16)

    high, low = composed(block_high), composed(block_low)
    high_ref[...] = high
    low_ref[...] = low
    out_ref[...] = split_product(high, low, values)


def coarse_kernel(high_ref, low_ref, values_ref, out_ref):
    out_ref[...] = split_product(high_ref[...], low_ref[...], values_ref[...])


def lift_kernel(inverse_ref, basis_ref, returned_ref, residual_ref, out_ref):
    members, tiles, share, tile = out_ref.shape
    rows_total = residual_ref.shape[1]
    residual = residual_ref[...]
    half = 0.25 * row_product(residual, inverse_ref[...])
    half = half + row_product(jnp.transpose(returned_ref[...]), basis_ref[...])
    for p, t in each_tile(members, rows_total // tile):
        out_ref[p, t] = half[p * share : (p + 1) * share, t * tile : (t + 1) * tile]
    if tiles > rows_total // tile:
        sums = jnp.sum(residual * half, axis=1, keepdims=True)
        for p in range(members):
            mine = sums[p * share : (p + 1) * share]
            out_ref[p, tiles - 1] = jnp.broadcast_to(mine, (share, tile))


def partner_places(listed_ref, place_ref, partner_ref, members, tiles):
    for e, t in each_tile(members, tiles):
        place_ref[listed_ref[e, t] * members + e] = t
    for p, t in each_tile(members, tiles):
        e = listed_ref[p, t]
        partner_ref[p * tiles + t] = e * tiles + place_ref[p * members + e]


def partner_of(partner_ref, p, t, tiles):
    flat = partner_ref[p * tiles + t]
    return lax.div(flat, tiles), lax.rem(flat, tiles)


def share_sums(value, share):
    rows = jnp.sum(value, axis=1, keepdims=True)
    return jnp.sum(rows.reshape(value.shape[0] // share, share, 1), axis=0)


def operate_kernel(
    listed_ref,
    incoming_ref,
    schur_ref,
    scale_ref,
    vector_ref,
    image_ref,
    out_ref,
    energy_ref,
    first_ref,
    partner_ref,
    place_ref,
    tiles_ref,
):
    members, tiles, share, tile = out_ref.shape
    partner_places(listed_ref, place_ref, partner_ref, members, tiles)
    for p, t in each_tile(members, tiles):
        other = incoming_ref[partner_of(partner_ref, p, t, tiles)]
        block(vector_ref, p, t, share, tile)[...] = incoming_ref[p, t] + other
    vector = vector_ref[...]
    image = scale_ref[:, 0:1] * row_product(vector, schur_ref[...])
    image_ref[...] = image
    for p, t in each_tile(members, tiles):
        tiles_ref[p, t] = image[p * share : (p + 1) * share, t * tile : (t + 1) * tile]
    for p, t in each_tile(members, tiles):
        out_ref[p, t] = tiles_ref[p, t] + tiles_ref[partner_of(partner_ref, p, t, tiles)]
    energy_ref[...] = jnp.sum(incoming_ref[:, tiles], axis=0)
    first_ref[...] = jnp.broadcast_to(share_sums(vector * image, share), first_ref.shape)


def entries_of(rows, columns, share, q):
    lane = lax.broadcasted_iota(jnp.int32, (rows, columns), 1)
    return lane == q * share + lax.broadcasted_iota(jnp.int32, (rows, columns), 0)


def last_kernel(
    partner_ref,
    incoming_ref,
    schur_ref,
    scale_ref,
    image_ref,
    energy_ref,
    first_ref,
    vector_ref,
    out_ref,
):
    members, tiles, share, tile = incoming_ref.shape
    for p, t in each_tile(members, tiles):
        other = incoming_ref[partner_of(partner_ref, p, t, tiles)]
        block(vector_ref, p, t, share, tile)[...] = incoming_ref[p, t] + other
    vector = vector_ref[...]
    product_rows = scale_ref[:, 0:1] * row_product(vector, schur_ref[...])
    sums = (
        energy_ref[:, 0:1],
        first_ref[:, 0:1],
        share_sums(vector * image_ref[...], share),
        share_sums(vector * product_rows, share),
    )
    columns = out_ref.shape[1]
    packed = jnp.zeros((share, columns), F32)
    for q, value in enumerate(sums):
        packed = jnp.where(entries_of(share, columns, share, q), value, packed)
    row = jnp.sum(packed, axis=0, keepdims=True)
    out_ref[...] = jnp.broadcast_to(row, out_ref.shape)


def combine_kernel(sums_ref, first_ref, second_ref, out_ref):
    members, tiles, share, tile = out_ref.shape
    columns = sums_ref.shape[1]
    row = jnp.sum(sums_ref[...], axis=0, keepdims=True)

    def total(q):
        mine = jnp.where(entries_of(share, columns, share, q), row, 0.0)
        return jnp.sum(mine, axis=1, keepdims=True)

    energy, gram_first, gram_mixed, gram_second = (total(q) for q in range(4))
    step_first = energy / gram_first
    mixed_share = gram_mixed / gram_first
    step_second = (gram_mixed - gram_first / energy * gram_first) / (
        gram_second - mixed_share * gram_mixed
    )
    along_first = step_first + step_second * (step_first * mixed_share)
    along_second = step_second * step_first
    for p, t in each_tile(members, tiles):
        here = block(first_ref, p, t, share, tile)[...]
        there = block(second_ref, p, t, share, tile)[...]
        out_ref[p, t] = along_first * here - along_second * there


def finish_kernel(incoming_ref, out_ref):
    members, tiles, share, tile = incoming_ref.shape
    for t in range(tiles):
        rows = incoming_ref[:, t].reshape(members * share, tile)
        out_ref[t * tile : (t + 1) * tile] = jnp.transpose(rows)


def call(kernel, scalars, inputs, outputs, flops=0, in_specs=None, out_specs=None, scratch_shapes=()):
    moved = sum(x.size * x.dtype.itemsize for x in inputs)
    moved += sum(x.size * x.dtype.itemsize for x in outputs)
    single = len(outputs) == 1
    specs = out_specs or [VMEM] * len(outputs)
    return pl.pallas_call(
        kernel,
        out_shape=outputs[0] if single else tuple(outputs),
        in_specs=in_specs or [SMEM] * len(scalars) + [VMEM] * len(inputs),
        out_specs=specs[0] if single else tuple(specs),
        scratch_shapes=scratch_shapes,
        compiler_params=pltpu.CompilerParams(vmem_limit_bytes=20 << 20),
        cost_estimate=pl.CostEstimate(flops=flops, bytes_accessed=moved, transcendentals=0),
    )(*scalars, *inputs)


def body(
    loads,
    coefficient,
    schur_ref,
    schur_inverse,
    coarse_basis,
    partners,
    routes,
    coarse_rows,
    primal_count,
    coarse_inverse,
):
    rows_total, columns = loads.shape[2:]
    peers = partners[0, 0]
    tile_count = peers.shape[1]
    tile = rows_total // tile_count
    members = lax.axis_size("dom")
    groups = lax.axis_size("sub")
    primal_max = coarse_basis.shape[3]
    cap = max(2, (primal_max + groups - 1) // groups)
    stride = cap + 1
    slots = groups * cap
    load_tiles = loads[0, 0]
    inverse_local = schur_inverse[0, 0]

    def shaped(*shape, dtype=F32):
        return jax.ShapeDtypeStruct(shape, dtype)

    share = columns // members
    vector_shape = shaped(columns, rows_total)
    slot_shape = shaped(slots, columns)
    tiles_shape = shaped(members, tile_count, share, tile)
    sum_shape = shaped(share, tile)
    big = 4 * rows_total * rows_total * columns
    thin = 4 * rows_total * slots * columns

    plane = rotated(members, middle_of_plane(members))
    ring = rotated(groups, groups // 2)

    def exchange(tiles):
        return lax.all_to_all(tiles, "dom", 0, 0, tiled=True, axis_index_groups=[plane])

    def shift(values, per_group):
        grouped = values.reshape(groups, 1, per_group * columns)
        moved = lax.all_to_all(grouped, "sub", 0, 0, tiled=True, axis_index_groups=[ring])
        return moved.reshape(groups * per_group, columns)

    given = [
        peers,
        routes.reshape(1, primal_max),
        coarse_rows[0],
        load_tiles,
        coarse_basis[0, 0].T,
    ]
    listed = [pltpu.SMEM(peers.shape, peers.dtype)]
    listed += [pltpu.VMEM(x.shape, x.dtype) for x in given]
    outgoing, slot_basis, wide_basis, labels = call(
        functools.partial(first_kernel, cap),
        [primal_count, coefficient],
        [pltpu.with_memory_space_constraint(x, pltpu.HBM) for x in given],
        [
            shaped(members, tile + 8, columns),
            shaped(slots, rows_total, dtype=BF16),
            shaped(groups * stride, rows_total, dtype=BF16),
            shaped(groups * stride, columns),
        ],
        thin,
        in_specs=[SMEM] * 2 + [pl.BlockSpec(memory_space=pltpu.HBM)] * len(given),
        scratch_shapes=listed
        + [pltpu.VMEM((8, columns), F32), pltpu.SemaphoreType.DMA((len(given) + 1,))],
    )
    residual, outgoing, listed, scale = call(
        first_residual_kernel,
        [peers],
        [load_tiles, exchange(outgoing), wide_basis, labels],
        [
            vector_shape,
            shaped(groups * stride, columns),
            shaped(members, columns, dtype=jnp.int32),
            shaped(columns, columns),
        ],
        2 * thin,
        scratch_shapes=[pltpu.VMEM((rows_total, columns), F32)],
    )
    arrived = shift(outgoing, stride)
    high, low, answer = call(
        functools.partial(first_coarse_kernel, cap, stride),
        [],
        [arrived, coarse_inverse[0, 0]],
        [shaped(slots, slots, dtype=BF16), shaped(slots, slots, dtype=BF16), slot_shape],
        20 * slots * slots * columns,
    )
    returned = shift(answer, cap)
    outgoing = call(
        lift_kernel,
        [],
        [inverse_local, slot_basis, returned, residual],
        [shaped(members, tile_count + 1, share, tile)],
        big + thin,
    )
    first, image, outgoing, energy, gram_first, partner = call(
        operate_kernel,
        [listed],
        [exchange(outgoing), schur_ref, scale],
        [
            vector_shape,
            vector_shape,
            tiles_shape,
            sum_shape,
            sum_shape,
            shaped(members * tile_count, dtype=jnp.int32),
        ],
        big,
        out_specs=[VMEM] * 5 + [SMEM],
        scratch_shapes=[
            pltpu.SMEM((members * members,), jnp.int32),
            pltpu.VMEM(tiles_shape.shape, F32),
        ],
    )
    residual, outgoing = call(
        residual_kernel, [], [exchange(outgoing), slot_basis], [vector_shape, slot_shape], thin
    )
    arrived = shift(outgoing, cap)
    answer = call(coarse_kernel, [], [high, low, arrived], [slot_shape], 6 * slots * slots * columns)
    returned = shift(answer, cap)
    outgoing = call(
        lift_kernel,
        [],
        [inverse_local, slot_basis, returned, residual],
        [tiles_shape],
        big + thin,
    )
    second, sums = call(
        last_kernel,
        [partner],
        [exchange(outgoing), schur_ref, scale, image, energy, gram_first],
        [vector_shape, shaped(groups, columns)],
        big,
    )
    outgoing = call(combine_kernel, [], [shift(sums, 1), first, second], [tiles_shape])
    solution = call(finish_kernel, [], [exchange(outgoing)], [shaped(rows_total, columns)])
    return solution.reshape(1, 1, rows_total, columns)


def solution(mesh):
    return jax.shard_map(
        body,
        mesh=mesh,
        in_specs=(
            P("sub", "dom", None, None),
            P("sub", "dom"),
            P(),
            P("sub", "dom", None, None),
            P("sub", "dom", None, None),
            P("sub", "dom", None, None),
            P("sub", "dom", None, None),
            P("sub", "dom", None),
            P("sub", "dom"),
            P("sub", "dom", None, None),
        ),
        out_specs=P("sub", "dom", None, None),
        check_vma=False,
    )
```

time: 266 us -> 254 us (0.955)
  blocking collectives: 254 us -> 241 us
    all_to_all x2 -> x0, blocking collectives: 38.4 us -> none  [gather(): lax.all_to_all(values, ('sub', 'dom'), 0, 0, tiled=True, axis_index_group...]
    all_to_all x4 -> x5, blocking collectives: 142 us -> 169 us  [shift(): lax.all_to_all(grouped, 'sub', 0, 0, tiled=True, axis_index_groups=[ring])]
    all_to_all x4 -> x5, blocking collectives: 73.1 us -> 71.7 us  [exchange(): lax.all_to_all(tiles, 'dom', 0, 0, tiled=True, axis_index_groups=[plane])]
where the time goes in v5:
time: 254 us
  blocking collectives  241 us (95%)
  Pallas kernels  11.1 us (4%)
    all_to_all x5, blocking collectives, shift(): lax.all_to_all(grouped, 'sub', 0, 0, tiled=True, axis_index_groups=[ring])  169 us
    all_to_all x5, blocking collectives, exchange(): lax.all_to_all(tiles, 'dom', 0, 0, tiled=True, axis_index_groups=[plane])  71.7 us
    pallas_call x11, Pallas kernels, call(): pl.pallas_call(kernel, out_shape=outputs[0] if single else tuple(outputs)...  11.1 us

profile of v5, /device:TPU:1, one launch (start us, length us, event | category | flops | bytes accessed | tf_op | source)
XLA Modules:
  0.0 253.6 jit_solution(12639826043122347742)
XLA Ops:
  0.0 0.0 copy-start.3
  0.0 0.0 copy-start.2
  1.4 1.7 shard_map.100
  3.1 0.0 copy-start.4
  3.1 0.0 copy-start
  3.1 16.5 %all_to_all.50.incoming_ref = f32[16,136,128]{2,1,0:T(8,128)S(1)} all-to-all(f32[16,136,128]{2,1,0:T(8,128)S(1)} %get-tuple-element.26), channel_id=1, replica_groups={{10,11,12,13,14,15,0,1,2,3,4,5,6,7,8,9},{26,27,28,29,30,31,16,17,18,19,..., dimensions={0} | all-to-all | bytes 2228224 | tf_op jit(solution)/shard_map/all_to_all | solution.py:405
  19.6 0.0 copy-done.3
  19.6 0.0 copy-done.2
  19.6 0.9 shard_map.101
  20.5 52.0 %all_to_all.51 = f32[64,1,384]{2,1,0:T(1,128)S(1)} all-to-all(f32[64,1,384]{2,1,0:T(1,128)S(1)} %bitcast.31), channel_id=1, replica_groups={{512,528,544,560,576,592,608,624,640,656,672,688,704,720,736,752,768,78..., dimensions={0} | all-to-all | bytes 196608 | tf_op jit(solution)/shard_map/all_to_all | solution.py:409
  72.5 0.0 copy-done.4
  72.5 0.6 shard_map.102
  73.1 30.1 %all_to_all.52 = f32[64,1,256]{2,1,0:T(1,128)S(1)} all-to-all(f32[64,1,256]{2,1,0:T(1,128)S(1)} %bitcast.33), channel_id=1, replica_groups={{512,528,544,560,576,592,608,624,640,656,672,688,704,720,736,752,768,78..., dimensions={0} | all-to-all | bytes 131072 | tf_op jit(solution)/shard_map/all_to_all | solution.py:409
  103.2 0.0 copy-done
  103.2 0.0 copy-start.1
  103.2 0.9 shard_map.103
  104.2 15.2 %all_to_all.53.incoming_ref = f32[16,9,8,128]{3,2,1,0:T(8,128)S(1)} all-to-all(f32[16,9,8,128]{3,2,1,0:T(8,128)S(1)} %shard_map.103), channel_id=1, replica_groups={{10,11,12,13,14,15,0,1,2,3,4,5,6,7,8,9},{26,27,28,29,30,31,16,17,18,19,..., dimensions={0} | all-to-all | bytes 1179648 | tf_op jit(solution)/shard_map/all_to_all | solution.py:405
  119.4 0.0 copy-done.1
  119.4 2.7 %shard_map.104 = (f32[128,1024]{1,0:T(8,128)S(1)}, f32[128,1024]{1,0:T(8,128)S(1)}, f32[16,8,8,128]{3,2,1,0:T(8,128)S(1)}, f32[8,128]{1,0:T(8,128)S(1)}, f32[8,128]{1,0:T(8,128)S(1)}, /*index=5*/s32[128]{0:T(128)S(1)}) custom-call(s32[16,128]{1,0:T(8,128)S(1)} %get-tuple-element.29.listed_ref, f32[16,9,8,128]{3,2,1,0:T(8,128)S(1)} %all_to_all.53.incoming_ref, ...), custom_call_target="tpu_custom_call" | custom-call | flops 536870912 | bytes 4334080 | tf_op jit(solution)/shard_map/pallas_call | solution.py:354
  122.1 13.1 %all_to_all.54.incoming_ref = f32[16,8,8,128]{3,2,1,0:T(8,128)S(1)} all-to-all(f32[16,8,8,128]{3,2,1,0:T(8,128)S(1)} %get-tuple-element.38), channel_id=1, replica_groups={{10,11,12,13,14,15,0,1,2,3,4,5,6,7,8,9},{26,27,28,29,30,31,16,17,18,19,..., dimensions={0} | all-to-all | bytes 1048576 | tf_op jit(solution)/shard_map/all_to_all | solution.py:405
  135.2 0.4 shard_map.105
  135.6 30.2 %all_to_all.55 = f32[64,1,256]{2,1,0:T(1,128)S(1)} all-to-all(f32[64,1,256]{2,1,0:T(1,128)S(1)} %bitcast.34), channel_id=1, replica_groups={{512,528,544,560,576,592,608,624,640,656,672,688,704,720,736,752,768,78..., dimensions={0} | all-to-all | bytes 131072 | tf_op jit(solution)/shard_map/all_to_all | solution.py:409
  165.8 0.2 shard_map.106
  166.0 30.2 %all_to_all.56 = f32[64,1,256]{2,1,0:T(1,128)S(1)} all-to-all(f32[64,1,256]{2,1,0:T(1,128)S(1)} %bitcast.29), channel_id=1, replica_groups={{512,528,544,560,576,592,608,624,640,656,672,688,704,720,736,752,768,78..., dimensions={0} | all-to-all | bytes 131072 | tf_op jit(solution)/shard_map/all_to_all | solution.py:409
  196.2 0.9 shard_map.107
  197.0 13.5 %all_to_all.57.incoming_ref = f32[16,8,8,128]{3,2,1,0:T(8,128)S(1)} all-to-all(f32[16,8,8,128]{3,2,1,0:T(8,128)S(1)} %shard_map.107), channel_id=1, replica_groups={{10,11,12,13,14,15,0,1,2,3,4,5,6,7,8,9},{26,27,28,29,30,31,16,17,18,19,..., dimensions={0} | all-to-all | bytes 1048576 | tf_op jit(solution)/shard_map/all_to_all | solution.py:405
  210.5 1.6 shard_map.108
  212.2 26.9 %all_to_all.58 = f32[64,1,128]{2,1,0:T(1,128)S(1)} all-to-all(f32[64,1,128]{2,1,0:T(1,128)S(1)} %bitcast.35), channel_id=1, replica_groups={{512,528,544,560,576,592,608,624,640,656,672,688,704,720,736,752,768,78..., dimensions={0} | all-to-all | bytes 65536 | tf_op jit(solution)/shard_map/all_to_all | solution.py:409
  239.1 0.2 shard_map.109
  239.3 13.3 %all_to_all.59.incoming_ref = f32[16,8,8,128]{3,2,1,0:T(8,128)S(1)} all-to-all(f32[16,8,8,128]{3,2,1,0:T(8,128)S(1)} %shard_map.109), channel_id=1, replica_groups={{10,11,12,13,14,15,0,1,2,3,4,5,6,7,8,9},{26,27,28,29,30,31,16,17,18,19,..., dimensions={0} | all-to-all | bytes 1048576 | tf_op jit(solution)/shard_map/all_to_all | solution.py:405
  252.6 1.0 shard_map.110
Async XLA Ops:
  0.0 19.6 %copy-start.3 = (s32[1,1,2,8]{3,2,1,0:T(2,128)S(1)}, s32[1,1,2,8]{3,2,1,0:T(2,128)}, u32[]{:S(2)}) copy-start(s32[1,1,2,8]{3,2,1,0:T(2,128)} %param.15) | copy-start | bytes 196
  0.0 19.6 %copy-start.2 = (f32[1,1,1024,128]{3,2,1,0:T(8,128)S(1)}, f32[1,1,1024,128]{3,2,1,0:T(8,128)}, u32[]{:S(2)}) copy-start(f32[1,1,1024,128]{3,2,1,0:T(8,128)} %param.10) | copy-start | bytes 1572868
  3.1 69.4 %copy-start.4 = (f32[1,1,64,64]{3,2,1,0:T(8,128)S(1)}, f32[1,1,64,64]{3,2,1,0:T(8,128)}, u32[]{:S(2)}) copy-start(f32[1,1,64,64]{3,2,1,0:T(8,128)} %param.19) | copy-start | bytes 49156
  3.1 100.1 %copy-start = (bf16[1,1,1024,1024]{3,2,1,0:T(8,128)(2,1)S(1)}, bf16[1,1,1024,1024]{3,2,1,0:T(8,128)(2,1)}, u32[]{:S(2)}) copy-start(bf16[1,1,1024,1024]{3,2,1,0:T(8,128)(2,1)} %param.13) | copy-start | bytes 6291460
  103.2 16.2 %copy-start.1 = (bf16[1024,1024]{1,0:T(8,128)(2,1)S(1)}, bf16[1024,1024]{1,0:T(8,128)(2,1)}, u32[]{:S(2)}) copy-start(bf16[1024,1024]{1,0:T(8,128)(2,1)} %schur_ref.3) | copy-start | bytes 6291460

commit v6 on v5

--- a/solution.py
+++ b/solution.py
@@ -79,8 +79,8 @@
     about_ref,
     semaphores,
 ):
-    sources = (peers_hbm, peers_hbm, routes_hbm, rows_hbm, loads_hbm, basis_hbm)
-    targets = (peers_ref, listed_ref, routes_ref, rows_ref, loads_ref, basis_ref)
+    sources = (peers_hbm, peers_hbm, routes_hbm, rows_hbm, basis_hbm, loads_hbm)
+    targets = (peers_ref, listed_ref, routes_ref, rows_ref, basis_ref, loads_ref)
     copies = [
         pltpu.make_async_copy(source, target, semaphores.at[i])
         for i, (source, target) in enumerate(zip(sources, targets))
@@ -88,17 +88,12 @@
     for copy in copies:
         copy.start()
     about_ref[...] = jnp.full_like(about_ref, stiffness_ref[0, 0])
-    for copy in copies:
-        copy.wait()
     tile_count = listed_ref.shape[1]
     tile = loads_ref.shape[0] // tile_count
     members = out_ref.shape[0]
-    about_ref[0:1, 0:tile_count] = listed_ref[0:1, :].astype(F32)
     out_ref[:, 0:tile] = jnp.zeros((members, tile, out_ref.shape[2]), F32)
-    for m in range(members):
-        out_ref[m, tile:] = about_ref[...]
-    for t in range(tile_count):
-        out_ref[place_of(peers_ref, t, members), 0:tile] = loads_ref[t * tile : (t + 1) * tile]
+    for copy in copies[2:5]:
+        copy.wait()
     groups = slot_basis_ref.shape[0] // cap
     target = lax.rem(routes_ref[...] + (groups - groups // 2), groups)
     listed = target.shape[1]
@@ -128,6 +123,13 @@
         found = jnp.sum(jnp.where(index == wanted, label, 0), axis=1, keepdims=True)
         labels = jnp.where(lane == i, found.astype(F32), labels)
     labels_ref[...] = labels
+    for copy in copies[:2] + copies[5:]:
+        copy.wait()
+    about_ref[0:1, 0:tile_count] = listed_ref[0:1, :].astype(F32)
+    for m in range(members):
+        out_ref[m, tile:] = about_ref[...]
+    for t in range(tile_count):
+        out_ref[place_of(peers_ref, t, members), 0:tile] = loads_ref[t * tile : (t + 1) * tile]
 
 
 def first_residual_kernel(
@@ -138,9 +140,10 @@
     labels_ref,
     residual_ref,
     out_ref,
-    listed_ref,
+    partner_ref,
     scale_ref,
     sum_ref,
+    listed_ref,
 ):
     members = incoming_ref.shape[0]
     columns, rows_total = residual_ref.shape
@@ -158,6 +161,7 @@
         listed_ref[m : m + 1] = lax.rem(listed + turn, members)
         stiffness = incoming_ref[m, tile + 1 : tile + 2]
         scale_ref[m * share : (m + 1) * share] = jnp.broadcast_to(stiffness, (share, columns))
+    partner_ref[...] = partner_places(listed_ref[...], peers_ref.shape[1])
 
 
 def residual_kernel(incoming_ref, basis_ref, residual_ref, out_ref):
@@ -220,29 +224,36 @@
 def lift_kernel(inverse_ref, basis_ref, returned_ref, residual_ref, out_ref):
     members, tiles, share, tile = out_ref.shape
     rows_total = residual_ref.shape[1]
-    residual = residual_ref[...]
-    half = 0.25 * row_product(residual, inverse_ref[...])
+    half = 0.25 * row_product(residual_ref[...], inverse_ref[...])
     half = half + row_product(jnp.transpose(returned_ref[...]), basis_ref[...])
     for p, t in each_tile(members, rows_total // tile):
         out_ref[p, t] = half[p * share : (p + 1) * share, t * tile : (t + 1) * tile]
     if tiles > rows_total // tile:
-        sums = jnp.sum(residual * half, axis=1, keepdims=True)
+        sums = jnp.sum(residual_ref[...] * half, axis=1, keepdims=True)
         for p in range(members):
             mine = sums[p * share : (p + 1) * share]
             out_ref[p, tiles - 1] = jnp.broadcast_to(mine, (share, tile))
 
 
-def partner_places(listed_ref, place_ref, partner_ref, members, tiles):
-    for e, t in each_tile(members, tiles):
-        place_ref[listed_ref[e, t] * members + e] = t
-    for p, t in each_tile(members, tiles):
-        e = listed_ref[p, t]
-        partner_ref[p * tiles + t] = e * tiles + place_ref[p * members + e]
+def partner_places(listed, tiles):
+    members = listed.shape[0]
+    lane = lax.broadcasted_iota(jnp.int32, listed.shape, 1)
+    member = lax.broadcasted_iota(jnp.int32, listed.shape, 0)
+    empty = jnp.zeros((listed.shape[1] - members, listed.shape[1]), F32)
+    across = jnp.transpose(jnp.concatenate([listed.astype(F32), empty], axis=0)).astype(jnp.int32)
+    found = jnp.zeros(listed.shape, jnp.int32)
+    for t in range(tiles):
+        found = jnp.where(across[t : t + 1] == member, t, found)
+    places = listed
+    for t in range(tiles):
+        mine = jnp.where(lane == listed[:, t : t + 1], found, 0)
+        place = jnp.sum(mine, axis=1, keepdims=True)
+        places = jnp.where(lane == tiles + t, place, places)
+    return places
 
 
 def partner_of(partner_ref, p, t, tiles):
-    flat = partner_ref[p * tiles + t]
-    return lax.div(flat, tiles), lax.rem(flat, tiles)
+    return partner_ref[p, t], partner_ref[p, tiles + t]
 
 
 def share_sums(value, share):
@@ -251,7 +262,7 @@
 
 
 def operate_kernel(
-    listed_ref,
+    partner_ref,
     incoming_ref,
     schur_ref,
     scale_ref,
@@ -260,12 +271,9 @@
     out_ref,
     energy_ref,
     first_ref,
-    partner_ref,
-    place_ref,
     tiles_ref,
 ):
     members, tiles, share, tile = out_ref.shape
-    partner_places(listed_ref, place_ref, partner_ref, members, tiles)
     for p, t in each_tile(members, tiles):
         other = incoming_ref[partner_of(partner_ref, p, t, tiles)]
         block(vector_ref, p, t, share, tile)[...] = incoming_ref[p, t] + other
@@ -433,7 +441,7 @@
         scratch_shapes=listed
         + [pltpu.VMEM((8, columns), F32), pltpu.SemaphoreType.DMA((len(given) + 1,))],
     )
-    residual, outgoing, listed, scale = call(
+    residual, outgoing, partner, scale = call(
         first_residual_kernel,
         [peers],
         [load_tiles, exchange(outgoing), wide_basis, labels],
@@ -444,7 +452,10 @@
             shaped(columns, columns),
         ],
         2 * thin,
-        scratch_shapes=[pltpu.VMEM((rows_total, columns), F32)],
+        scratch_shapes=[
+            pltpu.VMEM((rows_total, columns), F32),
+            pltpu.VMEM((members, columns), jnp.int32),
+        ],
     )
     arrived = shift(outgoing, stride)
     high, low, answer = call(
@@ -462,9 +473,9 @@
         [shaped(members, tile_count + 1, share, tile)],
         big + thin,
     )
-    first, image, outgoing, energy, gram_first, partner = call(
+    first, image, outgoing, energy, gram_first = call(
         operate_kernel,
-        [listed],
+        [partner],
         [exchange(outgoing), schur_ref, scale],
         [
             vector_shape,
@@ -472,14 +483,9 @@
             tiles_shape,
             sum_shape,
             sum_shape,
-            shaped(members * tile_count, dtype=jnp.int32),
         ],
         big,
-        out_specs=[VMEM] * 5 + [SMEM],
-        scratch_shapes=[
-            pltpu.SMEM((members * members,), jnp.int32),
-            pltpu.VMEM(tiles_shape.shape, F32),
-        ],
+        scratch_shapes=[pltpu.VMEM(tiles_shape.shape, F32)],
     )
     residual, outgoing = call(
         residual_kernel, [], [exchange(outgoing), slot_basis], [vector_shape, slot_shape], thin

time: 254 us -> 253 us (level)
  no operation moved by 1% of the time
where the time goes in v6:
time: 253 us; the launch traced here: 252 us
  blocking collectives  241 us (95%)
  Pallas kernels  10 us (4%)
    all_to_all x5, blocking collectives, shift(): lax.all_to_all(grouped, 'sub', 0, 0, tiled=True, axis_index_groups=[ring])  169 us
    all_to_all x5, blocking collectives, exchange(): lax.all_to_all(tiles, 'dom', 0, 0, tiled=True, axis_index_groups=[plane])  71.6 us
    pallas_call x11, Pallas kernels, call(): pl.pallas_call(kernel, out_shape=outputs[0] if single else tuple(outputs)...  10 us

profile of v6, /device:TPU:1, one launch (start us, length us, event | category | flops | bytes accessed | tf_op | source)
XLA Modules:
  0.0 252.4 jit_solution(11942753248793119938)
XLA Ops:
  0.0 0.0 copy-start.3
  0.0 0.0 copy-start.2
  1.4 1.5 shard_map.100
  2.9 0.0 copy-start.4
  2.9 0.0 copy-start
  2.9 16.5 %all_to_all.50.incoming_ref = f32[16,136,128]{2,1,0:T(8,128)S(1)} all-to-all(f32[16,136,128]{2,1,0:T(8,128)S(1)} %get-tuple-element.25), channel_id=1, replica_groups={{10,11,12,13,14,15,0,1,2,3,4,5,6,7,8,9},{26,27,28,29,30,31,16,17,18,19,..., dimensions={0} | all-to-all | bytes 2228224 | tf_op jit(solution)/shard_map/all_to_all | solution.py:413
  19.4 0.0 copy-done.3
  19.4 0.0 copy-done.2
  19.4 1.3 shard_map.101
  20.8 52.0 %all_to_all.51 = f32[64,1,384]{2,1,0:T(1,128)S(1)} all-to-all(f32[64,1,384]{2,1,0:T(1,128)S(1)} %bitcast.31), channel_id=1, replica_groups={{512,528,544,560,576,592,608,624,640,656,672,688,704,720,736,752,768,78..., dimensions={0} | all-to-all | bytes 196608 | tf_op jit(solution)/shard_map/all_to_all | solution.py:417
  72.8 0.0 copy-done.4
  72.8 0.6 shard_map.102
  73.4 30.1 %all_to_all.52 = f32[64,1,256]{2,1,0:T(1,128)S(1)} all-to-all(f32[64,1,256]{2,1,0:T(1,128)S(1)} %bitcast.33), channel_id=1, replica_groups={{512,528,544,560,576,592,608,624,640,656,672,688,704,720,736,752,768,78..., dimensions={0} | all-to-all | bytes 131072 | tf_op jit(solution)/shard_map/all_to_all | solution.py:417
  103.5 0.0 copy-done
  103.5 0.0 copy-start.1
  103.5 0.9 shard_map.103
  104.4 15.2 %all_to_all.53.incoming_ref = f32[16,9,8,128]{3,2,1,0:T(8,128)S(1)} all-to-all(f32[16,9,8,128]{3,2,1,0:T(8,128)S(1)} %shard_map.103), channel_id=1, replica_groups={{10,11,12,13,14,15,0,1,2,3,4,5,6,7,8,9},{26,27,28,29,30,31,16,17,18,19,..., dimensions={0} | all-to-all | bytes 1179648 | tf_op jit(solution)/shard_map/all_to_all | solution.py:413
  119.7 0.0 copy-done.1
  119.7 1.6 shard_map.104
  121.3 13.1 %all_to_all.54.incoming_ref = f32[16,8,8,128]{3,2,1,0:T(8,128)S(1)} all-to-all(f32[16,8,8,128]{3,2,1,0:T(8,128)S(1)} %get-tuple-element.36), channel_id=1, replica_groups={{10,11,12,13,14,15,0,1,2,3,4,5,6,7,8,9},{26,27,28,29,30,31,16,17,18,19,..., dimensions={0} | all-to-all | bytes 1048576 | tf_op jit(solution)/shard_map/all_to_all | solution.py:413
  134.3 0.4 shard_map.105
  134.7 30.1 %all_to_all.55 = f32[64,1,256]{2,1,0:T(1,128)S(1)} all-to-all(f32[64,1,256]{2,1,0:T(1,128)S(1)} %bitcast.34), channel_id=1, replica_groups={{512,528,544,560,576,592,608,624,640,656,672,688,704,720,736,752,768,78..., dimensions={0} | all-to-all | bytes 131072 | tf_op jit(solution)/shard_map/all_to_all | solution.py:417
  164.8 0.2 shard_map.106
  165.0 30.2 %all_to_all.56 = f32[64,1,256]{2,1,0:T(1,128)S(1)} all-to-all(f32[64,1,256]{2,1,0:T(1,128)S(1)} %bitcast.29), channel_id=1, replica_groups={{512,528,544,560,576,592,608,624,640,656,672,688,704,720,736,752,768,78..., dimensions={0} | all-to-all | bytes 131072 | tf_op jit(solution)/shard_map/all_to_all | solution.py:417
  195.1 0.8 shard_map.107
  196.0 13.5 %all_to_all.57.incoming_ref = f32[16,8,8,128]{3,2,1,0:T(8,128)S(1)} all-to-all(f32[16,8,8,128]{3,2,1,0:T(8,128)S(1)} %shard_map.107), channel_id=1, replica_groups={{10,11,12,13,14,15,0,1,2,3,4,5,6,7,8,9},{26,27,28,29,30,31,16,17,18,19,..., dimensions={0} | all-to-all | bytes 1048576 | tf_op jit(solution)/shard_map/all_to_all | solution.py:413
  209.5 1.5 shard_map.108
  211.0 27.0 %all_to_all.58 = f32[64,1,128]{2,1,0:T(1,128)S(1)} all-to-all(f32[64,1,128]{2,1,0:T(1,128)S(1)} %bitcast.35), channel_id=1, replica_groups={{512,528,544,560,576,592,608,624,640,656,672,688,704,720,736,752,768,78..., dimensions={0} | all-to-all | bytes 65536 | tf_op jit(solution)/shard_map/all_to_all | solution.py:417
  237.9 0.2 shard_map.109
  238.1 13.3 %all_to_all.59.incoming_ref = f32[16,8,8,128]{3,2,1,0:T(8,128)S(1)} all-to-all(f32[16,8,8,128]{3,2,1,0:T(8,128)S(1)} %shard_map.109), channel_id=1, replica_groups={{10,11,12,13,14,15,0,1,2,3,4,5,6,7,8,9},{26,27,28,29,30,31,16,17,18,19,..., dimensions={0} | all-to-all | bytes 1048576 | tf_op jit(solution)/shard_map/all_to_all | solution.py:413
  251.4 1.0 shard_map.110
Async XLA Ops:
  0.0 19.4 %copy-start.3 = (s32[1,1,2,8]{3,2,1,0:T(2,128)S(1)}, s32[1,1,2,8]{3,2,1,0:T(2,128)}, u32[]{:S(2)}) copy-start(s32[1,1,2,8]{3,2,1,0:T(2,128)} %param.15) | copy-start | bytes 196
  0.0 19.4 %copy-start.2 = (f32[1,1,1024,128]{3,2,1,0:T(8,128)S(1)}, f32[1,1,1024,128]{3,2,1,0:T(8,128)}, u32[]{:S(2)}) copy-start(f32[1,1,1024,128]{3,2,1,0:T(8,128)} %param.10) | copy-start | bytes 1572868
  2.9 69.9 %copy-start.4 = (f32[1,1,64,64]{3,2,1,0:T(8,128)S(1)}, f32[1,1,64,64]{3,2,1,0:T(8,128)}, u32[]{:S(2)}) copy-start(f32[1,1,64,64]{3,2,1,0:T(8,128)} %param.19) | copy-start | bytes 49156
  2.9 100.6 %copy-start = (bf16[1,1,1024,1024]{3,2,1,0:T(8,128)(2,1)S(1)}, bf16[1,1,1024,1024]{3,2,1,0:T(8,128)(2,1)}, u32[]{:S(2)}) copy-start(bf16[1,1,1024,1024]{3,2,1,0:T(8,128)(2,1)} %param.13) | copy-start | bytes 6291460
  103.5 16.2 %copy-start.1 = (bf16[1024,1024]{1,0:T(8,128)(2,1)S(1)}, bf16[1024,1024]{1,0:T(8,128)(2,1)}, u32[]{:S(2)}) copy-start(bf16[1024,1024]{1,0:T(8,128)(2,1)} %schur_ref.3) | copy-start | bytes 6291460

commit v7 on v6

--- a/solution.py
+++ b/solution.py
@@ -140,10 +140,9 @@
     labels_ref,
     residual_ref,
     out_ref,
-    partner_ref,
+    listed_ref,
     scale_ref,
     sum_ref,
-    listed_ref,
 ):
     members = incoming_ref.shape[0]
     columns, rows_total = residual_ref.shape
@@ -161,7 +160,6 @@
         listed_ref[m : m + 1] = lax.rem(listed + turn, members)
         stiffness = incoming_ref[m, tile + 1 : tile + 2]
         scale_ref[m * share : (m + 1) * share] = jnp.broadcast_to(stiffness, (share, columns))
-    partner_ref[...] = partner_places(listed_ref[...], peers_ref.shape[1])
 
 
 def residual_kernel(incoming_ref, basis_ref, residual_ref, out_ref):
@@ -250,6 +248,13 @@
         place = jnp.sum(mine, axis=1, keepdims=True)
         places = jnp.where(lane == tiles + t, place, places)
     return places
+
+
+def first_lift_kernel(
+    inverse_ref, basis_ref, returned_ref, residual_ref, listed_ref, out_ref, partner_ref
+):
+    partner_ref[...] = partner_places(listed_ref[...], out_ref.shape[1] - 1)
+    lift_kernel(inverse_ref, basis_ref, returned_ref, residual_ref, out_ref)
 
 
 def partner_of(partner_ref, p, t, tiles):
@@ -441,7 +446,7 @@
         scratch_shapes=listed
         + [pltpu.VMEM((8, columns), F32), pltpu.SemaphoreType.DMA((len(given) + 1,))],
     )
-    residual, outgoing, partner, scale = call(
+    residual, outgoing, listed, scale = call(
         first_residual_kernel,
         [peers],
         [load_tiles, exchange(outgoing), wide_basis, labels],
@@ -452,10 +457,7 @@
             shaped(columns, columns),
         ],
         2 * thin,
-        scratch_shapes=[
-            pltpu.VMEM((rows_total, columns), F32),
-            pltpu.VMEM((members, columns), jnp.int32),
-        ],
+        scratch_shapes=[pltpu.VMEM((rows_total, columns), F32)],
     )
     arrived = shift(outgoing, stride)
     high, low, answer = call(
@@ -466,11 +468,14 @@
         20 * slots * slots * columns,
     )
     returned = shift(answer, cap)
-    outgoing = call(
-        lift_kernel,
+    outgoing, partner = call(
+        first_lift_kernel,
         [],
-        [inverse_local, slot_basis, returned, residual],
-        [shaped(members, tile_count + 1, share, tile)],
+        [inverse_local, slot_basis, returned, residual, listed],
+        [
+            shaped(members, tile_count + 1, share, tile),
+            shaped(members, columns, dtype=jnp.int32),
+        ],
         big + thin,
     )
     first, image, outgoing, energy, gram_first = call(

time: 253 us -> 253 us (level)
  no operation moved by 1% of the time
where the time goes in v7:
time: 253 us; the launch traced here: 252 us
  blocking collectives  241 us (95%)
  Pallas kernels  9.59 us (4%)
    all_to_all x5, blocking collectives, shift(): lax.all_to_all(grouped, 'sub', 0, 0, tiled=True, axis_index_groups=[ring])  169 us
    all_to_all x5, blocking collectives, exchange(): lax.all_to_all(tiles, 'dom', 0, 0, tiled=True, axis_index_groups=[plane])  71.7 us
    pallas_call x11, Pallas kernels, call(): pl.pallas_call(kernel, out_shape=outputs[0] if single else tuple(outputs)...  9.59 us

profile of v7, /device:TPU:1, one launch (start us, length us, event | category | flops | bytes accessed | tf_op | source)
XLA Modules:
  0.0 252.1 jit_solution(17714372502129697716)
XLA Ops:
  0.0 0.0 copy-start.3
  0.0 0.0 copy-start.2
  1.4 1.5 shard_map.100
  2.9 0.0 copy-start.4
  2.9 0.0 copy-start
  2.9 16.5 %all_to_all.50.incoming_ref = f32[16,136,128]{2,1,0:T(8,128)S(1)} all-to-all(f32[16,136,128]{2,1,0:T(8,128)S(1)} %get-tuple-element.28), channel_id=1, replica_groups={{10,11,12,13,14,15,0,1,2,3,4,5,6,7,8,9},{26,27,28,29,30,31,16,17,18,19,..., dimensions={0} | all-to-all | bytes 2228224 | tf_op jit(solution)/shard_map/all_to_all | solution.py:418
  19.4 0.0 copy-done.3
  19.4 0.0 copy-done.2
  19.4 0.8 shard_map.101
  20.3 52.0 %all_to_all.51 = f32[64,1,384]{2,1,0:T(1,128)S(1)} all-to-all(f32[64,1,384]{2,1,0:T(1,128)S(1)} %bitcast.31), channel_id=1, replica_groups={{512,528,544,560,576,592,608,624,640,656,672,688,704,720,736,752,768,78..., dimensions={0} | all-to-all | bytes 196608 | tf_op jit(solution)/shard_map/all_to_all | solution.py:422
  72.3 0.0 copy-done.4
  72.3 0.6 shard_map.102
  73.0 30.1 %all_to_all.52 = f32[64,1,256]{2,1,0:T(1,128)S(1)} all-to-all(f32[64,1,256]{2,1,0:T(1,128)S(1)} %bitcast.33), channel_id=1, replica_groups={{512,528,544,560,576,592,608,624,640,656,672,688,704,720,736,752,768,78..., dimensions={0} | all-to-all | bytes 131072 | tf_op jit(solution)/shard_map/all_to_all | solution.py:422
  103.0 0.0 copy-start.1
  103.0 0.0 copy-done
  103.0 0.9 shard_map.103
  104.0 15.2 %all_to_all.53.incoming_ref = f32[16,9,8,128]{3,2,1,0:T(8,128)S(1)} all-to-all(f32[16,9,8,128]{3,2,1,0:T(8,128)S(1)} %get-tuple-element.38), channel_id=1, replica_groups={{10,11,12,13,14,15,0,1,2,3,4,5,6,7,8,9},{26,27,28,29,30,31,16,17,18,19,..., dimensions={0} | all-to-all | bytes 1179648 | tf_op jit(solution)/shard_map/all_to_all | solution.py:418
  119.2 0.0 copy-done.1
  119.2 1.6 shard_map.104
  120.8 13.1 %all_to_all.54.incoming_ref = f32[16,8,8,128]{3,2,1,0:T(8,128)S(1)} all-to-all(f32[16,8,8,128]{3,2,1,0:T(8,128)S(1)} %get-tuple-element.40), channel_id=1, replica_groups={{10,11,12,13,14,15,0,1,2,3,4,5,6,7,8,9},{26,27,28,29,30,31,16,17,18,19,..., dimensions={0} | all-to-all | bytes 1048576 | tf_op jit(solution)/shard_map/all_to_all | solution.py:418
  133.9 0.4 shard_map.105
  134.3 30.2 %all_to_all.55 = f32[64,1,256]{2,1,0:T(1,128)S(1)} all-to-all(f32[64,1,256]{2,1,0:T(1,128)S(1)} %bitcast.34), channel_id=1, replica_groups={{512,528,544,560,576,592,608,624,640,656,672,688,704,720,736,752,768,78..., dimensions={0} | all-to-all | bytes 131072 | tf_op jit(solution)/shard_map/all_to_all | solution.py:422
  164.5 0.2 shard_map.106
  164.6 30.2 %all_to_all.56 = f32[64,1,256]{2,1,0:T(1,128)S(1)} all-to-all(f32[64,1,256]{2,1,0:T(1,128)S(1)} %bitcast.29), channel_id=1, replica_groups={{512,528,544,560,576,592,608,624,640,656,672,688,704,720,736,752,768,78..., dimensions={0} | all-to-all | bytes 131072 | tf_op jit(solution)/shard_map/all_to_all | solution.py:422
  194.8 0.8 shard_map.107
  195.7 13.5 %all_to_all.57.incoming_ref = f32[16,8,8,128]{3,2,1,0:T(8,128)S(1)} all-to-all(f32[16,8,8,128]{3,2,1,0:T(8,128)S(1)} %shard_map.107), channel_id=1, replica_groups={{10,11,12,13,14,15,0,1,2,3,4,5,6,7,8,9},{26,27,28,29,30,31,16,17,18,19,..., dimensions={0} | all-to-all | bytes 1048576 | tf_op jit(solution)/shard_map/all_to_all | solution.py:418
  209.2 1.5 shard_map.108
  210.7 26.9 %all_to_all.58 = f32[64,1,128]{2,1,0:T(1,128)S(1)} all-to-all(f32[64,1,128]{2,1,0:T(1,128)S(1)} %bitcast.35), channel_id=1, replica_groups={{512,528,544,560,576,592,608,624,640,656,672,688,704,720,736,752,768,78..., dimensions={0} | all-to-all | bytes 65536 | tf_op jit(solution)/shard_map/all_to_all | solution.py:422
  237.6 0.2 shard_map.109
  237.8 13.3 %all_to_all.59.incoming_ref = f32[16,8,8,128]{3,2,1,0:T(8,128)S(1)} all-to-all(f32[16,8,8,128]{3,2,1,0:T(8,128)S(1)} %shard_map.109), channel_id=1, replica_groups={{10,11,12,13,14,15,0,1,2,3,4,5,6,7,8,9},{26,27,28,29,30,31,16,17,18,19,..., dimensions={0} | all-to-all | bytes 1048576 | tf_op jit(solution)/shard_map/all_to_all | solution.py:418
  251.1 1.0 shard_map.110
Async XLA Ops:
  0.0 19.4 %copy-start.3 = (s32[1,1,2,8]{3,2,1,0:T(2,128)S(1)}, s32[1,1,2,8]{3,2,1,0:T(2,128)}, u32[]{:S(2)}) copy-start(s32[1,1,2,8]{3,2,1,0:T(2,128)} %param.15) | copy-start | bytes 196
  0.0 19.4 %copy-start.2 = (f32[1,1,1024,128]{3,2,1,0:T(8,128)S(1)}, f32[1,1,1024,128]{3,2,1,0:T(8,128)}, u32[]{:S(2)}) copy-start(f32[1,1,1024,128]{3,2,1,0:T(8,128)} %param.10) | copy-start | bytes 1572868
  2.9 69.4 %copy-start.4 = (f32[1,1,64,64]{3,2,1,0:T(8,128)S(1)}, f32[1,1,64,64]{3,2,1,0:T(8,128)}, u32[]{:S(2)}) copy-start(f32[1,1,64,64]{3,2,1,0:T(8,128)} %param.19) | copy-start | bytes 49156
  2.9 100.1 %copy-start = (bf16[1,1,1024,1024]{3,2,1,0:T(8,128)(2,1)S(1)}, bf16[1,1,1024,1024]{3,2,1,0:T(8,128)(2,1)}, u32[]{:S(2)}) copy-start(bf16[1,1,1024,1024]{3,2,1,0:T(8,128)(2,1)} %param.13) | copy-start | bytes 6291460
  103.0 16.2 %copy-start.1 = (bf16[1024,1024]{1,0:T(8,128)(2,1)S(1)}, bf16[1024,1024]{1,0:T(8,128)(2,1)}, u32[]{:S(2)}) copy-start(bf16[1024,1024]{1,0:T(8,128)(2,1)} %schur_ref.3) | copy-start | bytes 6291460
